TPU v7x, 512 devices: a whole 4x4x16 slice. The times are simulated.
512 devices in a mesh: tm: 128 (over z, x_lo, y), space: 4 (over x_hi, core).
Axes of the slice: x: 4 (x_hi: 2, x_lo: 2; x = x_hi * 2 + x_lo), y: 4, z: 16, core: 2. Of those that a mesh axis runs over, the one named last changes fastest.
Arguments:
- initial_state: float32 [64, 1024], P(None, 'space'), may hold values from -4 to 4
- inv_mass: float32 [1024], P('space'), may hold values from 0.5 to 1
- element_scale: float32 [1024], P('space'), may hold values from 0.7 to 1.4
- mode_rate: float32 [128, 64], P('tm'), may hold values from 0.0005 to 1.2
- volume_block: bfloat16 [64, 64], replicated, may hold values from -0.0046 to 0.0016
- face_blocks: bfloat16 [6, 64, 64], replicated, may hold values from -0.0016 to 0.0046
Outputs:
- slice_end: float32 [128, 64, 1024], P('tm', None, 'space')
- first_guess: float32 [128, 64, 1024], P('tm', None, 'space')
All inputs are finite; a program needn't handle non-finite values.
Results may differ from a plain program's by a relative error of at most 0.0003.
Values may be sent and summed in bfloat16 or wider, within the bound.
A program may use at most 64 MiB of HBM per device.

v0:
```python
import jax
import jax.numpy as jnp
from jax import lax
from jax.sharding import PartitionSpec as P

DOF = 64
EY = 16
EZ = 8
FINE = 8
ITERS = 2


def with_halo(cells, sides, width):
    for axis, dim in sides:
        count = lax.axis_size(axis)
        ends = count - 1
        head = lax.slice_in_dim(cells, 0, width, axis=dim)
        tail = lax.slice_in_dim(cells, cells.shape[dim] - width, cells.shape[dim], axis=dim)
        cells = jnp.concatenate(
            [
                lax.ppermute(tail, axis, [(i, (i + 1) % count) for i in range(ends)]),
                cells,
                lax.ppermute(head, axis, [((i + 1) % count, i) for i in range(ends)]),
            ],
            axis=dim,
        )
    return cells


def carried_in(array, axis, combine, identity):
    peers, index = (lax.axis_size(axis), lax.axis_index(axis))
    everything = jax.tree.map(lambda part: lax.all_gather(part, axis), array)
    start = jax.tree.map(
        lambda part, zero: jnp.broadcast_to(jnp.asarray(zero, part.dtype), part.shape),
        array,
        identity,
    )

    def hop(k, before):
        reached = k < index
        new = combine(before, jax.tree.map(lambda part: part[k], everything))
        return jax.tree.map(lambda a, b: jnp.where(reached, a, b), new, before)

    return lax.fori_loop(0, peers, hop, start)


def operator_terms(padded, all_blocks):
    layer_size = EY * EZ
    cell_count = padded.shape[1] - 2 * layer_size
    centre = padded[:, layer_size : layer_size + cell_count]
    behind = padded[:, :cell_count]
    in_front = padded[:, 2 * layer_size :]
    shaped = centre.reshape(DOF, cell_count // layer_size, EY, EZ)
    south_side = jnp.roll(shaped, 1, axis=2).reshape(DOF, cell_count)
    north_side = jnp.roll(shaped, -1, axis=2).reshape(DOF, cell_count)
    lower_side = jnp.roll(shaped, 1, axis=3).reshape(DOF, cell_count)
    upper_side = jnp.roll(shaped, -1, axis=3).reshape(DOF, cell_count)
    stacked = jnp.concatenate(
        [centre, behind, in_front, south_side, north_side, lower_side, upper_side], axis=0
    )
    return jnp.dot(all_blocks, stacked, preferred_element_type=jnp.float32)


def add_rates(earlier_part, later_part):
    return earlier_part + later_part


def multiply_chain(earlier_part, later_part):
    return (earlier_part[0] * later_part[0], later_part[0] * earlier_part[1] + later_part[1])


def per_device(initial_state, inv_mass, element_scale, mode_rate, volume_block, face_blocks):
    layer_size = EY * EZ
    rate_row = mode_rate[0]
    scaled = rate_row[:, None] * element_scale[None, :]
    slice_decay = jnp.exp(-scaled)
    step_decay = jnp.exp(-scaled / FINE)
    mass_row = inv_mass[None, :]
    all_blocks = jnp.concatenate(
        [volume_block] + [face_blocks[face_index] for face_index in range(6)], axis=1
    )
    passed = carried_in(rate_row, "tm", add_rates, jnp.zeros_like(rate_row))
    slice_start = jnp.exp(-(passed[:, None] * element_scale[None, :])) * initial_state
    first_guess = slice_start
    offset = jnp.zeros_like(slice_start)
    for sweep_index in range(ITERS):
        fine_state = slice_start
        for fine_step in range(FINE):
            rounded = fine_state.astype(jnp.bfloat16)
            padded = with_halo(rounded, (("space", 1),), layer_size)
            fine_state = step_decay * fine_state + mass_row * operator_terms(padded, all_blocks)
        offset = fine_state - slice_decay * slice_start
        carried, summed = carried_in(
            (slice_decay, offset),
            "tm",
            multiply_chain,
            (jnp.ones_like(slice_decay), jnp.zeros_like(offset)),
        )
        slice_start = carried * initial_state + summed
    ending = slice_decay * slice_start + offset
    return (ending[None], first_guess[None])


def solution(mesh):
    placed = (P(None, "space"), P("space"), P("space"), P("tm", None), P(), P())
    return jax.shard_map(
        per_device,
        mesh=mesh,
        in_specs=placed,
        out_specs=(P("tm", None, "space"), P("tm", None, "space")),
        check_vma=False,
    )
```

profile of v0, /device:TPU:480, one launch (start us, length us, event | category | flops | bytes accessed | tf_op | source)
XLA Modules:
  0.0 2435.0 jit_solution(12250133577585457665)
XLA Ops:
  7.3 287.7 %all-gather.2 = f32[128,1,64]{2,1,0:T(1,128)S(1)} all-gather(f32[1,1,64]{2,1,0:T(1,128)} %bitcast.291), channel_id=1, replica_groups=mesh['tm'=128,'space'=4] {'tm'}, dimensions={0}, use_global_device_ids=true | all-gather | bytes 33024 | tf_op jit(solution)/shard_map/all_gather | solution.py:32
  294.9 5.2 while.46
  300.1 0.9 constant_dynamic-update-slice_fusion.6
  301.1 1.3 collective-permute-start
  302.4 1.3 collective-permute-start.1
  303.7 1.4 negate_exponential_fusion
  308.4 1.0 constant_dynamic-update-slice_fusion.13
  309.6 5.9 collective-permute-start.2
  315.5 1.3 collective-permute-start.3
  317.5 3.1 collective-permute-done.3
  321.7 5.9 collective-permute-start.4
  328.2 1.3 collective-permute-start.5
  329.6 1.8 collective-permute-done.5
  331.7 5.4 collective-permute-start.6
  337.8 1.3 collective-permute-start.7
  339.1 1.8 collective-permute-done.7
  341.2 5.4 collective-permute-start.8
  347.3 1.3 collective-permute-start.9
  348.6 1.8 collective-permute-done.9
  350.8 5.7 collective-permute-start.10
  357.1 1.3 collective-permute-start.11
  358.4 1.8 collective-permute-done.11
  360.5 5.4 collective-permute-start.12
  366.6 1.3 collective-permute-start.13
  367.9 1.8 collective-permute-done.13
  370.1 5.9 collective-permute-start.14
  376.6 1.3 collective-permute-start.15
  377.9 1.8 collective-permute-done.15
  380.6 527.4 %all-gather.7.cloned.1.call-done = f32[128,64,256]{2,1,0:T(8,128)} async-done(((f32[1,64,256]{2,1,0:T(8,128)}), f32[128,64,256]{2,1,0:T(8,128)}) %all-gather.7.cloned.1.call-update) | async-done | bytes 8388624 | tf_op jit(solution)/shard_map/all_gather | solution.py:32
  908.0 602.0 %all-gather.9.cloned.1.call-done = f32[8192,256]{1,0:T(8,128)} async-done(((f32[64,256]{1,0:T(8,128)}), f32[8192,256]{1,0:T(8,128)}) %all-gather.9.cloned.1.call-update) | async-done | bytes 8388624 | tf_op jit(solution)/shard_map/all_gather | solution.py:32
  1510.0 120.6 %while.47 = (s32[]{:T(128)}, f32[64,256]{1,0:T(8,128)S(1)}, f32[64,256]{1,0:T(8,128)S(1)}, s32[]{:T(128)}, f32[128,64,256]{2,1,0:T(8,128)}, /*index=5*/f32[128,64,256]{2,1,0:T(8,128)}, s32[]{:T(128)}, s32[]{:T(128)}) while((s32[]{:T(128)}, f32[64,256]{1,0:T(8,128)S(1)}, f32[64,256]{1,0:T(8,128)S(1)}, s32[]{:T(128)}, ...), condition=%wide.region_3.4_spmd.clone, body=%wide.region_2.3_spmd.clone.sunk | while | flops 114692 | bytes 393325 | solution.py:44
  1511.9 0.9 fusion.138
  1513.8 0.9 fusion.138
  1515.7 0.9 fusion.138
  1518.5 0.9 fusion.138
  1520.4 0.9 fusion.138
  1525.1 0.9 fusion.138
  1630.9 1.3 collective-permute-start.16
  1632.8 1.3 collective-permute-start.17
  1634.1 4.6 collective-permute-done.17
  1639.2 5.9 collective-permute-start.18
  1645.6 1.3 collective-permute-start.19
  1647.0 1.8 collective-permute-done.19
  1649.2 5.4 collective-permute-start.20
  1655.2 1.3 collective-permute-start.21
  1656.5 1.8 collective-permute-done.21
  1658.7 5.4 collective-permute-start.22
  1664.7 1.3 collective-permute-start.23
  1666.0 1.8 collective-permute-done.23
  1668.2 5.4 collective-permute-start.24
  1674.2 1.3 collective-permute-start.25
  1675.5 1.8 collective-permute-done.25
  1677.8 5.4 collective-permute-start.26
  1683.8 1.3 collective-permute-start.27
  1685.1 1.8 collective-permute-done.27
  1687.3 5.4 collective-permute-start.28
  1693.3 1.3 collective-permute-start.29
  1694.6 1.8 collective-permute-done.29
  1696.8 5.4 collective-permute-start.30
  1702.8 1.3 collective-permute-start.31
  1704.1 1.8 collective-permute-done.31
  1706.8 599.5 %all-gather.11.cloned.1.call-done = f32[8192,256]{1,0:T(8,128)} async-done(((f32[64,256]{1,0:T(8,128)}), f32[8192,256]{1,0:T(8,128)}) %all-gather.11.cloned.1.call-update) | async-done | bytes 8388624 | tf_op jit(solution)/shard_map/all_gather | solution.py:32
  2306.3 120.6 %while.48 = (s32[]{:T(128)}, f32[64,256]{1,0:T(8,128)S(1)}, f32[64,256]{1,0:T(8,128)S(1)}, s32[]{:T(128)}, f32[128,64,256]{2,1,0:T(8,128)}, /*index=5*/f32[128,64,256]{2,1,0:T(8,128)}, s32[]{:T(128)}, s32[]{:T(128)}) while((s32[]{:T(128)}, f32[64,256]{1,0:T(8,128)S(1)}, f32[64,256]{1,0:T(8,128)S(1)}, s32[]{:T(128)}, ...), condition=%wide.region_5.6_spmd.clone, body=%wide.region_4.5_spmd.clone.sunk | while | flops 114692 | bytes 393325 | solution.py:44
  2426.9 1.6 fusion.21
  (750 shorter events, 250.8 us)
Async XLA Ops:
  7.2 324.2 %copy-start.3 = (f32[1,64]{1,0:T(1,128)S(1)}, f32[1,64]{1,0:T(1,128)}, u32[]{:S(2)}) copy-start(f32[1,64]{1,0:T(1,128)} %param.15) | copy-start | bytes 772
  7.2 324.2 %copy-start.1 = (f32[256]{0:T(256)S(1)}, f32[256]{0:T(256)}, u32[]{:S(2)}) copy-start(f32[256]{0:T(256)} %param.14) | copy-start | bytes 3076
  7.2 324.2 %copy-start.2 = (f32[256]{0:T(256)S(1)}, f32[256]{0:T(256)}, u32[]{:S(2)}) copy-start(f32[256]{0:T(256)} %param.13) | copy-start | bytes 3076
  7.2 900.8 %all-gather.7.cloned.1.call-start = ((), (), s32[]{:S(2)}) async-start(), calls=%async_computation | async-start | bytes 8454144 | tf_op jit(solution)/shard_map/all_gather | solution.py:32
  301.1 6.5 collective-permute-start
  302.4 6.0 collective-permute-start.1
  305.1 1205.0 %all-gather.9.cloned.1.call-start = ((), (), s32[]{:S(2)}) async-start(), calls=%async_computation.1 | async-start | bytes 8454144 | tf_op jit(solution)/shard_map/all_gather | solution.py:32
  309.6 7.8 collective-permute-start.2
  315.5 5.1 collective-permute-start.3
  317.1 62.7 %copy-start = (f32[64,256]{1,0:T(8,128)S(1)}, f32[64,256]{1,0:T(8,128)}, u32[]{:S(2)}) copy-start(f32[64,256]{1,0:T(8,128)} %param.12) | copy-start | bytes 196612
  321.7 7.9 collective-permute-start.4
  328.2 3.1 collective-permute-start.5
  331.7 7.4 collective-permute-start.6
  337.8 3.1 collective-permute-start.7
  341.2 7.4 collective-permute-start.8
  347.3 3.1 collective-permute-start.9
  350.8 7.7 collective-permute-start.10
  357.1 3.1 collective-permute-start.11
  360.5 7.4 collective-permute-start.12
  366.6 3.1 collective-permute-start.13
  370.1 7.8 collective-permute-start.14
  376.6 3.1 collective-permute-start.15
  380.6 1925.7 %all-gather.11.cloned.1.call-start = ((), (), s32[]{:S(2)}) async-start(), calls=%async_computation.2 | async-start | bytes 8454144 | tf_op jit(solution)/shard_map/all_gather | solution.py:32
  1630.9 3.2 collective-permute-start.16
  1632.8 5.9 collective-permute-start.17
  1639.2 7.8 collective-permute-start.18
  1645.6 3.1 collective-permute-start.19
  1649.2 7.3 collective-permute-start.20
  1655.2 3.1 collective-permute-start.21
  1658.7 7.3 collective-permute-start.22
  1664.7 3.1 collective-permute-start.23
  1668.2 7.3 collective-permute-start.24
  1674.2 3.1 collective-permute-start.25
  1677.8 7.3 collective-permute-start.26
  1683.8 3.1 collective-permute-start.27
  1687.3 7.3 collective-permute-start.28
  1693.3 3.1 collective-permute-start.29
  1696.8 7.3 collective-permute-start.30
  1702.8 3.1 collective-permute-start.31
Sparse Core Ops, SparseCore 0:
  305.2 602.7 all-gather.6
  910.7 599.3 all-gather.8
  1706.9 599.3 all-gather.10
where the time goes:
time: 2470 us; the launch traced here: 2440 us
  waiting for transfers between devices  1760 us (71%)
  blocking collectives  288 us (12%)
  other arithmetic  244 us (10%)
  starting transfers between devices  101 us (4%)
    all_gather x3, waiting for transfers between devices, carried_in(): everything = jax.tree.map(lambda part: lax.all_gather(part, axis), array)  1730 us
    all_gather x1, blocking collectives, carried_in(): everything = jax.tree.map(lambda part: lax.all_gather(part, axis), array)  288 us
    select_n x384, other arithmetic, hop(): return jax.tree.map(lambda a, b: jnp.where(reached, a, b), new, before)  237 us
    ppermute x16, starting transfers between devices, with_halo(): lax.ppermute(tail, axis, [(i, (i + 1) % count) for i in range(ends)])  80.5 us
  transfers between devices with their start and end apart: 35, of which 19 were waited for; matrix products, arithmetic and copies ran while one was open for 1% of the time, Pallas kernels for 0%

commit v1 on v0

v1 whole, which is shorter than its diff:
```python
import functools

import jax
import jax.numpy as jnp
from jax import lax
from jax.experimental import pallas as pl
from jax.experimental.pallas import tpu as pltpu
from jax.sharding import PartitionSpec as P

DOF = 64
EY = 16
EZ = 8
FINE = 8
ITERS = 2
LAYER = EY * EZ
MESH = pl.DeviceIdType.MESH


def kernel(
    depth, plane, shards,
    init_ref, mass_ref, scale_ref, rate_ref, volume_ref, faces_ref,
    end_ref, guess_ref,
    blocks, state, decay, coarse, start, rounded, full, halo, rows, row_src,
    rate_src, plane_rates, tot_src, z_rates,
    plane_gain, z_gain, off_src, offs, sum_src, sums, back_src, back,
    rate_send, rate_recv, tot_send, tot_recv, halo_send, halo_recv, row_send, row_recv,
    off_send, off_recv, sum_send, sum_recv, back_send, back_recv,
):
    group = DOF // plane
    cells = init_ref.shape[1]
    time = lax.axis_index("tm")
    mine = lax.axis_index("space")
    z = time // plane
    j = lax.rem(time, plane)

    def plane_peer(q):
        return (z * plane + q, mine)

    def z_peer(k):
        return (k * plane + j, mine)

    def space_peer(p):
        return (time, p)

    def others(count, me, body):
        def step(d, carry):
            body(lax.rem(me + 1 + d, count))
            return carry

        lax.fori_loop(0, count - 1, step, 0)

    barrier = pltpu.get_barrier_semaphore()
    others(plane, j, lambda q: pl.semaphore_signal(barrier, inc=1, device_id=plane_peer(q), device_id_type=MESH))
    others(shards, mine, lambda p: pl.semaphore_signal(barrier, inc=1, device_id=space_peer(p), device_id_type=MESH))
    others(depth, z, lambda k: pl.semaphore_signal(barrier, inc=1, device_id=z_peer(k), device_id_type=MESH))

    blocks[:, :DOF] = volume_ref[...]
    for f in range(6):
        blocks[:, DOF * (f + 1) : DOF * (f + 2)] = faces_ref[f]
    zero_half = jnp.zeros((DOF, cells), jnp.bfloat16)
    rounded[0] = zero_half
    rounded[shards + 1] = zero_half
    row = jnp.concatenate([rate_ref[...], jnp.zeros((1, 128 - DOF), jnp.float32)], axis=1)
    rate_src[...] = row
    plane_rates[pl.ds(j, 1)] = row[None]
    row_src[...] = jnp.concatenate(
        [mass_ref[...], scale_ref[...], jnp.zeros((6, cells), jnp.float32)], axis=0
    )
    rows[pl.ds(mine, 1)] = row_src[...][None]
    full[pl.ds(mine, 1)] = init_ref[...][None]
    sub = lax.broadcasted_iota(jnp.int32, (DOF, 128), 0)
    lane = lax.broadcasted_iota(jnp.int32, (DOF, 128), 1)
    sub_g = lax.broadcasted_iota(jnp.int32, (group, 128), 0)
    lane_g = lax.broadcasted_iota(jnp.int32, (group, 128), 1)

    def column(values):
        return jnp.sum(jnp.where(sub == lane, values, 0.0), axis=1, keepdims=True)

    def group_column(values):
        return jnp.sum(jnp.where(lane_g == sub_g + group * j, values, 0.0), axis=1, keepdims=True)

    own_scale = scale_ref[...]
    own_column = column(row)
    coarse[...] = jnp.exp(-(own_column * own_scale))

    pl.semaphore_wait(barrier, plane + shards + depth - 3)

    def rate_copy(q):
        return pltpu.make_async_remote_copy(
            src_ref=rate_src, dst_ref=plane_rates.at[j], send_sem=rate_send.at[q], recv_sem=rate_recv.at[j],
            device_id=plane_peer(q), device_id_type=MESH)

    def rate_arrival(q):
        return pltpu.make_async_remote_copy(
            src_ref=rate_src, dst_ref=plane_rates.at[q], send_sem=rate_send.at[q], recv_sem=rate_recv.at[q],
            device_id=plane_peer(q), device_id_type=MESH)

    def full_copy(p, slot):
        return pltpu.make_async_remote_copy(
            src_ref=init_ref, dst_ref=full.at[slot], send_sem=halo_send.at[0, p],
            recv_sem=halo_recv.at[0, slot], device_id=space_peer(p), device_id_type=MESH)

    def halo_copy(it, p, slot):
        return pltpu.make_async_remote_copy(
            src_ref=halo.at[it - 1, mine], dst_ref=halo.at[it - 1, slot], send_sem=halo_send.at[it, p],
            recv_sem=halo_recv.at[it, slot], device_id=space_peer(p), device_id_type=MESH)

    def row_copy(p, slot):
        return pltpu.make_async_remote_copy(
            src_ref=row_src, dst_ref=rows.at[slot], send_sem=row_send.at[p],
            recv_sem=row_recv.at[slot], device_id=space_peer(p), device_id_type=MESH)

    others(plane, j, lambda q: rate_copy(q).start())
    others(shards, mine, lambda p: row_copy(p, mine).start())
    others(shards, mine, lambda p: full_copy(p, mine).start())
    others(plane, j, lambda q: rate_arrival(q).wait_recv())
    total = jnp.zeros((1, 128), jnp.float32)
    before = jnp.zeros((1, 128), jnp.float32)
    for q in range(plane):
        before = before + jnp.where(q < j, plane_rates[q], 0.0)
        total = total + plane_rates[q]
    tot_src[...] = total

    def tot_copy(k, slot):
        return pltpu.make_async_remote_copy(
            src_ref=tot_src, dst_ref=z_rates.at[slot], send_sem=tot_send.at[k], recv_sem=tot_recv.at[slot],
            device_id=z_peer(k), device_id_type=MESH)

    def later(body):
        lax.fori_loop(0, depth - 1 - z, lambda d, c: (body(depth - 1 - d), c)[1], 0)

    later(lambda k: tot_copy(k, z).start())

    for q in range(plane):
        plane_gain[q] = jnp.exp(-(group_column(plane_rates[q]) * own_scale))
    others(shards, mine, lambda p: row_copy(p, p).wait_recv())
    for p in range(shards):
        decay[p] = jnp.exp(-(own_column * rows[p, 1:2, :]) / FINE)
    others(shards, mine, lambda p: full_copy(p, p).wait_recv())

    def add_total(k, carried):
        tot_copy(k, k).wait_recv()
        return carried + z_rates[k]

    passed = column(lax.fori_loop(0, z, add_total, before))
    for p in range(shards):
        state[p] = jnp.exp(-(passed * rows[p, 1:2, :])) * full[p]
    guess = jnp.exp(-(passed * own_scale)) * init_ref[...]
    guess_ref[...] = guess
    start[...] = guess
    state[pl.ds(mine, 1)] = guess[None]

    lane_z = lax.rem(lax.broadcasted_iota(jnp.int32, (2 * DOF, LAYER), 1), EZ)
    at_low = lane_z == 0
    at_high = lane_z == EZ - 1

    def fine_step(step, carry):
        for p in range(shards):
            rounded[p + 1] = state[p].astype(jnp.bfloat16)
        for p in range(shards):
            centre = rounded[p + 1]
            behind = jnp.concatenate([rounded[p, :, LAYER:], rounded[p + 1, :, :LAYER]], axis=1)
            ahead = jnp.concatenate([rounded[p + 1, :, LAYER:], rounded[p + 2, :, :LAYER]], axis=1)
            tall = jnp.concatenate([state[p, :, :LAYER], state[p, :, LAYER:]], axis=0)
            south = pltpu.roll(tall, EZ, 1)
            north = pltpu.roll(tall, LAYER - EZ, 1)
            lower = jnp.where(at_low, pltpu.roll(tall, LAYER - EZ + 1, 1), pltpu.roll(tall, 1, 1))
            upper = jnp.where(at_high, pltpu.roll(tall, EZ - 1, 1), pltpu.roll(tall, LAYER - 1, 1))

            def wide(value):
                value = value.astype(jnp.bfloat16)
                return jnp.concatenate([value[:DOF], value[DOF:]], axis=1)

            stacked = jnp.concatenate(
                [centre, behind, ahead, wide(south), wide(north), wide(lower), wide(upper)], axis=0
            )
            change = jnp.dot(blocks[...], stacked, preferred_element_type=jnp.float32)
            state[p] = decay[p] * state[p] + rows[p, 0:1, :] * change
        return carry

    offset = None
    for it in range(ITERS):
        lax.fori_loop(0, FINE, fine_step, 0)
        offset = state[pl.ds(mine, 1)][0] - coarse[...] * start[...]
        for q in range(plane):
            off_src[q] = offset[q * group : (q + 1) * group]

        def off_copy(q, slot):
            return pltpu.make_async_remote_copy(
                src_ref=off_src.at[q], dst_ref=offs.at[it, slot], send_sem=off_send.at[it, q],
                recv_sem=off_recv.at[it, slot], device_id=plane_peer(q), device_id_type=MESH)

        others(plane, j, lambda q: off_copy(q, j).start())
        offs[it, pl.ds(j, 1)] = off_src[pl.ds(j, 1)]
        if it == 0:
            def fill_gain(k, carry):
                z_gain[k] = jnp.exp(-(group_column(z_rates[k]) * own_scale))
                return carry

            lax.fori_loop(0, z, fill_gain, 0)
        others(plane, j, lambda q: off_copy(q, q).wait_recv())
        part = offs[it, 0]
        for q in range(1, plane):
            part = plane_gain[q] * part + offs[it, q]
        sum_src[it] = part

        def sum_copy(k, slot):
            return pltpu.make_async_remote_copy(
                src_ref=sum_src.at[it], dst_ref=sums.at[it, slot], send_sem=sum_send.at[it, k],
                recv_sem=sum_recv.at[it, slot], device_id=z_peer(k), device_id_type=MESH)

        later(lambda k: sum_copy(k, z).start())

        def add_sum(k, carried):
            sum_copy(k, k).wait_recv()
            return z_gain[k] * carried + sums[it, k]

        carried = lax.fori_loop(0, z, add_sum, jnp.zeros((group, cells), jnp.float32))
        for q in range(plane):
            back_src[it, q] = carried
            carried = plane_gain[q] * carried + offs[it, q]

        def back_copy(q, slot):
            return pltpu.make_async_remote_copy(
                src_ref=back_src.at[it, q], dst_ref=back.at[it, slot], send_sem=back_send.at[it, q],
                recv_sem=back_recv.at[it, slot], device_id=plane_peer(q), device_id_type=MESH)

        others(plane, j, lambda q: back_copy(q, j).start())
        back[it, pl.ds(j, 1)] = back_src[it, pl.ds(j, 1)]
        others(plane, j, lambda q: off_copy(q, j).wait_send())
        later(lambda k: sum_copy(k, z).wait_send())
        others(plane, j, lambda q: back_copy(q, q).wait_recv())
        following = guess_ref[...] + back[it].reshape(DOF, cells)
        if it + 1 < ITERS:
            start[...] = following
            halo[it, pl.ds(mine, 1)] = following.astype(jnp.bfloat16)[None]
            others(shards, mine, lambda p: halo_copy(it + 1, p, mine).start())
            others(shards, mine, lambda p: halo_copy(it + 1, p, p).wait_recv())
            for p in range(shards):
                state[p] = halo[it, p].astype(jnp.float32)
            state[pl.ds(mine, 1)] = following[None]
        else:
            end_ref[...] = coarse[...] * following + offset
        others(plane, j, lambda q: back_copy(q, j).wait_send())

    others(plane, j, lambda q: rate_copy(q).wait_send())
    others(shards, mine, lambda p: row_copy(p, mine).wait_send())
    others(shards, mine, lambda p: full_copy(p, mine).wait_send())
    for it in range(1, ITERS):
        others(shards, mine, lambda p: halo_copy(it, p, mine).wait_send())
    later(lambda k: tot_copy(k, z).wait_send())


def per_device(depth, plane, initial_state, inv_mass, element_scale, mode_rate, volume_block, face_blocks):
    shards = lax.axis_size("space")
    cells = initial_state.shape[1]
    group = DOF // plane
    f32, bf16 = jnp.float32, jnp.bfloat16
    vmem = pl.BlockSpec(memory_space=pltpu.VMEM)
    dma = pltpu.SemaphoreType.DMA
    end, guess = pl.pallas_call(
        functools.partial(kernel, depth, plane, shards),
        out_shape=[jax.ShapeDtypeStruct((DOF, cells), f32)] * 2,
        in_specs=[vmem] * 6,
        out_specs=[vmem] * 2,
        scratch_shapes=[
            pltpu.VMEM((DOF, 7 * DOF), bf16),
            pltpu.VMEM((shards, DOF, cells), f32),
            pltpu.VMEM((shards, DOF, cells), f32),
            pltpu.VMEM((DOF, cells), f32),
            pltpu.VMEM((DOF, cells), f32),
            pltpu.VMEM((shards + 2, DOF, cells), bf16),
            pltpu.VMEM((shards, DOF, cells), f32),
            pltpu.VMEM((ITERS - 1, shards, DOF, cells), bf16),
            pltpu.VMEM((shards, 8, cells), f32),
            pltpu.VMEM((8, cells), f32),
            pltpu.VMEM((1, 128), f32),
            pltpu.VMEM((plane, 1, 128), f32),
            pltpu.VMEM((1, 128), f32),
            pltpu.VMEM((depth, 1, 128), f32),
            pltpu.VMEM((plane, group, cells), f32),
            pltpu.VMEM((depth, group, cells), f32),
            pltpu.VMEM((plane, group, cells), f32),
            pltpu.VMEM((ITERS, plane, group, cells), f32),
            pltpu.VMEM((ITERS, group, cells), f32),
            pltpu.VMEM((ITERS, depth, group, cells), f32),
            pltpu.VMEM((ITERS, plane, group, cells), f32),
            pltpu.VMEM((ITERS, plane, group, cells), f32),
            dma((plane,)), dma((plane,)), dma((depth,)), dma((depth,)),
            dma((ITERS, shards)), dma((ITERS, shards)), dma((shards,)), dma((shards,)),
            dma((ITERS, plane)), dma((ITERS, plane)), dma((ITERS, depth)), dma((ITERS, depth)),
            dma((ITERS, plane)), dma((ITERS, plane)),
        ],
        compiler_params=pltpu.CompilerParams(collective_id=1, has_side_effects=True, vmem_limit_bytes=32 << 20),
        name="parareal",
    )(initial_state, inv_mass[None], element_scale[None], mode_rate, volume_block, face_blocks)
    return end[None], guess[None]


def solution(mesh):
    slices = mesh.shape["tm"]
    plane = 8 if slices % 8 == 0 else 2
    placed = (P(None, "space"), P("space"), P("space"), P("tm", None), P(), P())
    return jax.shard_map(
        functools.partial(per_device, slices // plane, plane),
        mesh=mesh,
        in_specs=placed,
        out_specs=(P("tm", None, "space"), P("tm", None, "space")),
        check_vma=False,
    )
```

time: 2470 us -> 67.6 us (0.03); the launches traced: 2440 us -> 66.5 us
  waiting for transfers between devices: 1760 us -> 0 us
  blocking collectives: 288 us -> 0 us
  other arithmetic: 244 us -> 0 us
  starting transfers between devices: 101 us -> 0 us
  Pallas kernels: 0 us -> 61.4 us
    all_gather x3 -> x0, waiting for transfers between devices: 1730 us -> none  [carried_in(): everything = jax.tree.map(lambda part: lax.all_gather(part, axis), array)]
    all_gather x1 -> x0, blocking collectives: 288 us -> none  [carried_in(): everything = jax.tree.map(lambda part: lax.all_gather(part, axis), array)]
    select_n x384 -> x0, other arithmetic: 237 us -> none  [hop(): return jax.tree.map(lambda a, b: jnp.where(reached, a, b), new, before)]
    ppermute x32 -> x0, starting transfers between devices: 101 us -> none  [the longest x16 80.5 us: with_halo(): lax.ppermute(tail, axis, [(i, (i + 1) % count) for i in range(ends)])]
    pallas_call x0 -> x1, Pallas kernels: none -> 61.4 us  [per_device(): pl.pallas_call(functools.partial(kernel, depth, plane, shards), out_shape...]
    ppermute x32 -> x0, waiting for transfers between devices: 31.4 us -> none  [the longest x16 31.4 us: with_halo(): lax.ppermute(head, axis, [((i + 1) % count, i) for i in range(ends)])]
  transfers between devices with their start and end apart: 35 -> 0, of which waited for: 19 -> 0; matrix products, arithmetic and copies ran while one was open for 1% -> 0% of each run, Pallas kernels for 0% -> 0%
where the time goes in v1:
time: 67.6 us; the launch traced here: 66.5 us
  Pallas kernels  61.4 us (91%)
  local copies, waits for them, and re-layouts  4.38 us (6%)
    pallas_call x1, Pallas kernels, per_device(): pl.pallas_call(functools.partial(kernel, depth, plane, shards), out_shape...  61.4 us
    unnamed x14, local copies, waits for them, and re-layouts  4.38 us

profile of v1, /device:TPU:480, one launch (start us, length us, event | category | flops | bytes accessed | tf_op | source)
XLA Modules:
  0.0 66.5 jit_solution(12011841973146717106)
XLA Ops:
  0.6 0.0 copy-start.4
  0.6 0.0 copy-start.3
  0.7 0.0 copy-start.5
  0.7 0.7 copy-done.4
  1.3 0.0 copy-done.3
  1.3 0.0 copy-done.5
  1.3 0.0 copy-start
  1.3 0.9 %copy-done = bf16[6,64,64]{2,1,0:T(8,128)(2,1)S(1)} copy-done((bf16[6,64,64]{2,1,0:T(8,128)(2,1)S(1)}, bf16[6,64,64]{2,1,0:T(8,128)(2,1)}, u32[]{:S(2)}) %copy-start) | copy-done | bytes 49176
  2.2 0.0 copy-start.1
  2.2 0.8 %copy-done.1 = f32[64,256]{1,0:T(8,128)S(1)} copy-done((f32[64,256]{1,0:T(8,128)S(1)}, f32[64,256]{1,0:T(8,128)}, u32[]{:S(2)}) %copy-start.1) | copy-done | bytes 65560
  3.1 0.0 copy-start.2
  3.1 0.7 %copy-done.2 = bf16[64,64]{1,0:T(8,128)(2,1)S(1)} copy-done((bf16[64,64]{1,0:T(8,128)(2,1)S(1)}, bf16[64,64]{1,0:T(8,128)(2,1)}, u32[]{:S(2)}) %copy-start.2) | copy-done | bytes 8216
  3.8 61.4 %parareal.1 = (f32[64,256]{1,0:T(8,128)S(1)}, f32[64,256]{1,0:T(8,128)S(1)}) custom-call(f32[64,256]{1,0:T(8,128)S(1)} %copy-done.1, f32[1,256]{1,0:T(1,128)S(1)} %bitcast.6, f32[1,256]{1,0:T(1,128)S(1)} %bitcast.7, f32[1,64]{1,0:T(1,128)S(1)} %copy-done.5, bf16[64,64]{1,0:T(8,128)(2,1)S(1)} %copy-done.2, bf16[6,64,64]{2,1,0:T(8,128)(2,1)S(1)} %copy-done), custom_call_target="tpu_custom_call" | custom-call | tf_op jit(solution)/shard_map/parareal/pallas_call | solution.py:261
  65.2 0.6 copy.10
  65.9 0.6 copy.11
Async XLA Ops:
  0.6 0.7 %copy-start.4 = (f32[256]{0:T(256)S(1)}, f32[256]{0:T(256)}, u32[]{:S(2)}) copy-start(f32[256]{0:T(256)} %param.8) | copy-start | bytes 3076
  0.6 0.7 %copy-start.3 = (f32[256]{0:T(256)S(1)}, f32[256]{0:T(256)}, u32[]{:S(2)}) copy-start(f32[256]{0:T(256)} %param.7) | copy-start | bytes 3076
  0.7 0.7 %copy-start.5 = (f32[1,64]{1,0:T(1,128)S(1)}, f32[1,64]{1,0:T(1,128)}, u32[]{:S(2)}) copy-start(f32[1,64]{1,0:T(1,128)} %rate_ref.1) | copy-start | bytes 772
  1.3 0.9 %copy-start = (bf16[6,64,64]{2,1,0:T(8,128)(2,1)S(1)}, bf16[6,64,64]{2,1,0:T(8,128)(2,1)}, u32[]{:S(2)}) copy-start(bf16[6,64,64]{2,1,0:T(8,128)(2,1)} %faces_ref.1) | copy-start | bytes 147460
  2.2 0.8 %copy-start.1 = (f32[64,256]{1,0:T(8,128)S(1)}, f32[64,256]{1,0:T(8,128)}, u32[]{:S(2)}) copy-start(f32[64,256]{1,0:T(8,128)} %init_ref.1) | copy-start | bytes 196612
  3.1 0.7 %copy-start.2 = (bf16[64,64]{1,0:T(8,128)(2,1)S(1)}, bf16[64,64]{1,0:T(8,128)(2,1)}, u32[]{:S(2)}) copy-start(bf16[64,64]{1,0:T(8,128)(2,1)} %volume_ref.1) | copy-start | bytes 24580

commit v2 on v1

v2 whole, which is shorter than its diff:
```python
import functools

import jax
import jax.numpy as jnp
from jax import lax
from jax.experimental import pallas as pl
from jax.experimental.pallas import tpu as pltpu
from jax.sharding import PartitionSpec as P

DOF = 64
EY = 16
EZ = 8
FINE = 8
ITERS = 2
LAYER = EY * EZ
OCTET = 8
MESH = pl.DeviceIdType.MESH


def kernel(
    depth, group, shards,
    init_hbm, mass_hbm, scale_hbm, rate_hbm, volume_hbm, faces_hbm,
    end_ref, guess_ref,
    init_ref, mass_ref, scale_ref, rate_ref, volume_ref, faces_ref,
    blocks, state, decay, coarse, start, rounded, full, halo, rows, row_src,
    rate_src, group_rates, tot_src, z_rates,
    group_gain, z_gain, off_src, offs, sum_src, sums, back_src, back,
    load, rate_send, rate_recv, tot_send, tot_recv, full_send, full_recv, halo_send, halo_recv,
    row_send, row_recv, off_send, off_recv, sum_send, sum_recv, back_send, back_recv,
):
    cells = init_ref.shape[1]
    time = lax.axis_index("tm")
    mine = lax.axis_index("space")
    z = time // group
    j = lax.rem(time, group)

    def group_peer(q):
        return (z * group + q, mine)

    def z_peer(k):
        return (k * group + j, mine)

    def space_peer(p):
        return (time, p)

    def others(count, me, body):
        def step(d, carry):
            body(lax.rem(me + 1 + d, count))
            return carry

        lax.fori_loop(0, count - 1, step, 0)

    def later(body):
        lax.fori_loop(0, depth - 1 - z, lambda d, c: (body(depth - 1 - d), c)[1], 0)

    def greet(peer):
        pl.semaphore_signal(barrier, inc=1, device_id=peer, device_id_type=MESH)

    def arrived(ref, sem):
        pltpu.make_async_copy(ref, ref, sem).wait()

    barrier = pltpu.get_barrier_semaphore()
    lax.fori_loop(0, z, lambda k, c: (greet(z_peer(k)), c)[1], 0)
    others(group, j, lambda q: greet(group_peer(q)))
    others(shards, mine, lambda p: greet(space_peer(p)))

    loads = [
        pltpu.make_async_copy(src, dst, load.at[n])
        for n, (src, dst) in enumerate([
            (rate_hbm, rate_ref), (scale_hbm, scale_ref), (mass_hbm, mass_ref),
            (init_hbm, init_ref), (volume_hbm, volume_ref), (faces_hbm, faces_ref),
        ])
    ]
    for copy in loads:
        copy.start()

    zero_part = jnp.zeros((DOF, cells), jnp.bfloat16)
    rounded[0] = zero_part
    rounded[shards + 1] = zero_part
    sub = lax.broadcasted_iota(jnp.int32, (DOF, 128), 0)
    lane = lax.broadcasted_iota(jnp.int32, (DOF, 128), 1)
    sub_o = lax.broadcasted_iota(jnp.int32, (OCTET, 128), 0)
    lane_o = lax.broadcasted_iota(jnp.int32, (OCTET, 128), 1)
    first_mode = OCTET * (j // 2)

    def column(values):
        return jnp.sum(jnp.where(sub == lane, values, 0.0), axis=1, keepdims=True)

    def octet_column(values):
        return jnp.sum(jnp.where(lane_o == sub_o + first_mode, values, 0.0), axis=1, keepdims=True)

    for copy in loads:
        copy.wait()
    row = jnp.concatenate([rate_ref[...], jnp.zeros((1, 128 - DOF), jnp.float32)], axis=1)
    rate_src[...] = row
    group_rates[pl.ds(j, 1)] = row[None]
    row_src[...] = jnp.concatenate(
        [mass_ref[...], scale_ref[...], jnp.zeros((6, cells), jnp.float32)], axis=0
    )
    rows[pl.ds(mine, 1)] = row_src[...][None]
    full[pl.ds(mine, 1)] = init_ref[...][None]
    blocks[:, :DOF] = volume_ref[...]
    for f in range(6):
        blocks[:, DOF * (f + 1) : DOF * (f + 2)] = faces_ref[f]
    own_scale = scale_ref[...]
    half_scale = scale_ref[:, pl.ds(pl.multiple_of(LAYER * lax.rem(j, 2), LAYER), LAYER)]
    own_column = column(row)
    coarse[...] = jnp.exp(-(own_column * own_scale))

    pl.semaphore_wait(barrier, group + shards + depth - 3 - z)

    def rate_copy(q):
        return pltpu.make_async_remote_copy(
            src_ref=rate_src, dst_ref=group_rates.at[j], send_sem=rate_send, recv_sem=rate_recv,
            device_id=group_peer(q), device_id_type=MESH)

    def full_copy(p):
        return pltpu.make_async_remote_copy(
            src_ref=init_ref, dst_ref=full.at[mine], send_sem=full_send, recv_sem=full_recv,
            device_id=space_peer(p), device_id_type=MESH)

    def halo_copy(it, p):
        return pltpu.make_async_remote_copy(
            src_ref=halo.at[it, mine], dst_ref=halo.at[it, mine], send_sem=halo_send.at[it],
            recv_sem=halo_recv.at[it], device_id=space_peer(p), device_id_type=MESH)

    def row_copy(p):
        return pltpu.make_async_remote_copy(
            src_ref=row_src, dst_ref=rows.at[mine], send_sem=row_send, recv_sem=row_recv,
            device_id=space_peer(p), device_id_type=MESH)

    others(group, j, lambda q: rate_copy(q).start())
    others(shards, mine, lambda p: row_copy(p).start())
    others(shards, mine, lambda p: full_copy(p).start())
    arrived(group_rates.at[pl.ds(0, group - 1)], rate_recv)
    total = jnp.zeros((1, 128), jnp.float32)
    before = jnp.zeros((1, 128), jnp.float32)
    for q in range(group):
        before = before + jnp.where(q < j, group_rates[q], 0.0)
        total = total + group_rates[q]
    tot_src[...] = total

    def tot_copy(k, slot):
        return pltpu.make_async_remote_copy(
            src_ref=tot_src, dst_ref=z_rates.at[slot], send_sem=tot_send.at[k], recv_sem=tot_recv.at[slot],
            device_id=z_peer(k), device_id_type=MESH)

    later(lambda k: tot_copy(k, z).start())

    for q in range(group):
        group_gain[q] = jnp.exp(-(octet_column(group_rates[q]) * half_scale))
    arrived(rows.at[pl.ds(0, shards - 1)], row_recv)
    for p in range(shards):
        decay[p] = jnp.exp(-(own_column * rows[p, 1:2, :]) / FINE)
    arrived(full.at[pl.ds(0, shards - 1)], full_recv)

    def add_total(k, carried):
        tot_copy(k, k).wait_recv()
        return carried + z_rates[k]

    passed = column(lax.fori_loop(0, z, add_total, before))
    for p in range(shards):
        state[p] = jnp.exp(-(passed * rows[p, 1:2, :])) * full[p]
    guess = state[pl.ds(mine, 1)][0]
    guess_ref[...] = guess
    start[...] = guess

    lane_t = lax.broadcasted_iota(jnp.int32, (2 * DOF, LAYER), 1)
    lane_z = lax.rem(lane_t, EZ)
    lower_of = lane_t - lane_z + lax.rem(lane_z + EZ - 1, EZ)
    upper_of = lane_t - lane_z + lax.rem(lane_z + 1, EZ)

    def fine_step(step, carry):
        for p in range(shards):
            rounded[p + 1] = state[p].astype(jnp.bfloat16)
        for p in range(shards):
            centre = rounded[p + 1]
            behind = jnp.concatenate([rounded[p, :, LAYER:], rounded[p + 1, :, :LAYER]], axis=1)
            ahead = jnp.concatenate([rounded[p + 1, :, LAYER:], rounded[p + 2, :, :LAYER]], axis=1)
            tall = jnp.concatenate([state[p, :, :LAYER], state[p, :, LAYER:]], axis=0)
            south = pltpu.roll(tall, EZ, 1)
            north = pltpu.roll(tall, LAYER - EZ, 1)
            lower = jnp.take_along_axis(tall, lower_of, axis=1, mode="promise_in_bounds")
            upper = jnp.take_along_axis(tall, upper_of, axis=1, mode="promise_in_bounds")

            def wide(value):
                value = value.astype(jnp.bfloat16)
                return jnp.concatenate([value[:DOF], value[DOF:]], axis=1)

            stacked = jnp.concatenate(
                [centre, behind, ahead, wide(south), wide(north), wide(lower), wide(upper)], axis=0
            )
            change = jnp.dot(blocks[...], stacked, preferred_element_type=jnp.float32)
            state[p] = decay[p] * state[p] + rows[p, 0:1, :] * change
        return carry

    offset = None
    for it in range(ITERS):
        lax.fori_loop(0, FINE, fine_step, 0, unroll=FINE)
        offset = state[pl.ds(mine, 1)][0] - coarse[...] * start[...]
        for q in range(group):
            off_src[it, q] = offset[OCTET * (q // 2) : OCTET * (q // 2 + 1), LAYER * (q % 2) : LAYER * (q % 2 + 1)]

        def off_copy(q):
            return pltpu.make_async_remote_copy(
                src_ref=off_src.at[it, q], dst_ref=offs.at[it, j], send_sem=off_send.at[it],
                recv_sem=off_recv.at[it], device_id=group_peer(q), device_id_type=MESH)

        others(group, j, lambda q: off_copy(q).start())
        offs[it, pl.ds(j, 1)] = off_src[it, pl.ds(j, 1)]
        if it == 0:
            def fill_gain(k, carry):
                z_gain[k] = jnp.exp(-(octet_column(z_rates[k]) * half_scale))
                return carry

            lax.fori_loop(0, z, fill_gain, 0)
        arrived(offs.at[it, pl.ds(0, group - 1)], off_recv.at[it])
        part = offs[it, 0]
        for q in range(1, group):
            part = group_gain[q] * part + offs[it, q]
        sum_src[it] = part

        def sum_copy(k, slot):
            return pltpu.make_async_remote_copy(
                src_ref=sum_src.at[it], dst_ref=sums.at[it, slot], send_sem=sum_send.at[it, k],
                recv_sem=sum_recv.at[it, slot], device_id=z_peer(k), device_id_type=MESH)

        later(lambda k: sum_copy(k, z).start())

        def add_sum(k, carried):
            sum_copy(k, k).wait_recv()
            return z_gain[k] * carried + sums[it, k]

        carried = lax.fori_loop(0, z, add_sum, jnp.zeros((OCTET, LAYER), jnp.float32))
        for q in range(group):
            back_src[it, q] = carried
            carried = group_gain[q] * carried + offs[it, q]

        def back_copy(q):
            return pltpu.make_async_remote_copy(
                src_ref=back_src.at[it, q], dst_ref=back.at[it, j], send_sem=back_send.at[it],
                recv_sem=back_recv.at[it], device_id=group_peer(q), device_id_type=MESH)

        others(group, j, lambda q: back_copy(q).start())
        back[it, pl.ds(j, 1)] = back_src[it, pl.ds(j, 1)]
        arrived(back.at[it, pl.ds(0, group - 1)], back_recv.at[it])
        correction = jnp.concatenate(
            [jnp.concatenate([back[it, 2 * m], back[it, 2 * m + 1]], axis=1) for m in range(DOF // OCTET)], axis=0
        )
        following = guess_ref[...] + correction
        if it + 1 < ITERS:
            start[...] = following
            halo[it, pl.ds(mine, 1)] = following.astype(jnp.bfloat16)[None]
            others(shards, mine, lambda p: halo_copy(it, p).start())
            arrived(halo.at[it, pl.ds(0, shards - 1)], halo_recv.at[it])
            for p in range(shards):
                state[p] = halo[it, p].astype(jnp.float32)
            state[pl.ds(mine, 1)] = following[None]
        else:
            end_ref[...] = coarse[...] * following + offset

    def left(ref, sem):
        pltpu.make_async_copy(ref, ref, sem).wait()

    left(group_rates.at[pl.ds(0, group - 1)], rate_send)
    left(rows.at[pl.ds(0, shards - 1)], row_send)
    left(full.at[pl.ds(0, shards - 1)], full_send)
    later(lambda k: tot_copy(k, z).wait_send())
    for it in range(ITERS):
        left(off_src.at[it, pl.ds(0, group - 1)], off_send.at[it])
        left(back_src.at[it, pl.ds(0, group - 1)], back_send.at[it])
        if it + 1 < ITERS:
            left(halo.at[it, pl.ds(0, shards - 1)], halo_send.at[it])

        def summed(k):
            pltpu.make_async_copy(sum_src.at[it], sum_src.at[it], sum_send.at[it, k]).wait()

        later(summed)


def per_device(depth, group, initial_state, inv_mass, element_scale, mode_rate, volume_block, face_blocks):
    shards = lax.axis_size("space")
    cells = initial_state.shape[1]
    f32, bf16 = jnp.float32, jnp.bfloat16
    vmem = pl.BlockSpec(memory_space=pltpu.VMEM)
    hbm = pl.BlockSpec(memory_space=pltpu.HBM)
    dma = pltpu.SemaphoreType.DMA
    end, guess = pl.pallas_call(
        functools.partial(kernel, depth, group, shards),
        out_shape=[jax.ShapeDtypeStruct((DOF, cells), f32)] * 2,
        in_specs=[hbm] * 6,
        out_specs=[vmem] * 2,
        scratch_shapes=[
            pltpu.VMEM((DOF, cells), f32),
            pltpu.VMEM((1, cells), f32),
            pltpu.VMEM((1, cells), f32),
            pltpu.VMEM((1, DOF), f32),
            pltpu.VMEM((DOF, DOF), bf16),
            pltpu.VMEM((6, DOF, DOF), bf16),
            pltpu.VMEM((DOF, 7 * DOF), bf16),
            pltpu.VMEM((shards, DOF, cells), f32),
            pltpu.VMEM((shards, DOF, cells), f32),
            pltpu.VMEM((DOF, cells), f32),
            pltpu.VMEM((DOF, cells), f32),
            pltpu.VMEM((shards + 2, DOF, cells), bf16),
            pltpu.VMEM((shards, DOF, cells), f32),
            pltpu.VMEM((ITERS - 1, shards, DOF, cells), bf16),
            pltpu.VMEM((shards, 8, cells), f32),
            pltpu.VMEM((8, cells), f32),
            pltpu.VMEM((1, 128), f32),
            pltpu.VMEM((group, 1, 128), f32),
            pltpu.VMEM((1, 128), f32),
            pltpu.VMEM((depth, 1, 128), f32),
            pltpu.VMEM((group, OCTET, LAYER), f32),
            pltpu.VMEM((depth, OCTET, LAYER), f32),
            pltpu.VMEM((ITERS, group, OCTET, LAYER), f32),
            pltpu.VMEM((ITERS, group, OCTET, LAYER), f32),
            pltpu.VMEM((ITERS, OCTET, LAYER), f32),
            pltpu.VMEM((ITERS, depth, OCTET, LAYER), f32),
            pltpu.VMEM((ITERS, group, OCTET, LAYER), f32),
            pltpu.VMEM((ITERS, group, OCTET, LAYER), f32),
            dma((6,)), dma, dma, dma((depth,)), dma((depth,)),
            dma, dma, dma((ITERS,)), dma((ITERS,)),
            dma, dma, dma((ITERS,)), dma((ITERS,)),
            dma((ITERS, depth)), dma((ITERS, depth)), dma((ITERS,)), dma((ITERS,)),
        ],
        compiler_params=pltpu.CompilerParams(collective_id=1, has_side_effects=True),
        name="parareal",
    )(initial_state, inv_mass[None], element_scale[None], mode_rate, volume_block, face_blocks)
    return end[None], guess[None]


def solution(mesh):
    slices = mesh.shape["tm"]
    group = (DOF // OCTET) * 2
    placed = (P(None, "space"), P("space"), P("space"), P("tm", None), P(), P())
    return jax.shard_map(
        functools.partial(per_device, slices // group, group),
        mesh=mesh,
        in_specs=placed,
        out_specs=(P("tm", None, "space"), P("tm", None, "space")),
        check_vma=False,
    )
```

time: 67.6 us -> 60.6 us (0.90)
  Pallas kernels: 61.4 us -> 57.3 us
  local copies, waits for them, and re-layouts: 4.38 us -> 2.14 us
    pallas_call x1, Pallas kernels: 61.4 us -> 57.3 us  [per_device(): pl.pallas_call(functools.partial(kernel, depth, group, shards), out_shape...]
    unnamed x14 -> x4, local copies, waits for them, and re-layouts: 4.38 us -> 2.14 us
where the time goes in v2:
time: 60.6 us; the launch traced here: 60.1 us
  Pallas kernels  57.3 us (95%)
  local copies, waits for them, and re-layouts  2.14 us (4%)
  between operations  0.65 us (1%)
    pallas_call x1, Pallas kernels, per_device(): pl.pallas_call(functools.partial(kernel, depth, group, shards), out_shape...  57.3 us
    unnamed x4, local copies, waits for them, and re-layouts  2.14 us

profile of v2, /device:TPU:480, one launch (start us, length us, event | category | flops | bytes accessed | tf_op | source)
XLA Modules:
  0.0 60.1 jit_solution(4867390435774100752)
XLA Ops:
  0.6 57.3 %parareal.1 = (f32[64,256]{1,0:T(8,128)}, f32[64,256]{1,0:T(8,128)}) custom-call(f32[64,256]{1,0:T(8,128)} %init_hbm.1, f32[1,256]{1,0:T(1,128)} %bitcast.6, f32[1,256]{1,0:T(1,128)} %bitcast.7, f32[1,64]{1,0:T(1,128)} %rate_hbm.1, bf16[64,64]{1,0:T(8,128)(2,1)} %volume_hbm.1, bf16[6,64,64]{2,1,0:T(8,128)(2,1)} %faces_hbm.1), custom_call_target="tpu_custom_call" | custom-call | tf_op jit(solution)/shard_map/parareal/pallas_call | solution.py:288
  58.0 0.0 copy-start
  58.0 1.5 %copy.10 = f32[1,64,256]{2,1,0:T(8,128)} copy(f32[1,64,256]{2,1,0:T(8,128)} %bitcast.5) | data formatting | bytes 131072
  59.5 0.0 copy-done
  59.5 0.6 %copy.11 = f32[1,64,256]{2,1,0:T(8,128)} copy(f32[1,64,256]{2,1,0:T(8,128)S(1)} %bitcast.4) | data formatting | bytes 131072
Async XLA Ops:
  58.0 1.5 %copy-start = (f32[64,256]{1,0:T(8,128)S(1)}, f32[64,256]{1,0:T(8,128)}, u32[]{:S(2)}) copy-start(f32[64,256]{1,0:T(8,128)} %get-tuple-element.5) | copy-start | bytes 196612

commit v3 on v2

--- a/solution.py
+++ b/solution.py
@@ -14,18 +14,19 @@
 ITERS = 2
 LAYER = EY * EZ
 OCTET = 8
+NEAR = 2
 MESH = pl.DeviceIdType.MESH
 
 
 def kernel(
     depth, group, shards,
     init_hbm, mass_hbm, scale_hbm, rate_hbm, volume_hbm, faces_hbm,
-    end_ref, guess_ref,
+    sum_ref, difference_ref,
     init_ref, mass_ref, scale_ref, rate_ref, volume_ref, faces_ref,
-    blocks, state, decay, coarse, start, rounded, full, halo, rows, row_src,
-    rate_src, group_rates, tot_src, z_rates,
+    blocks, state, decay, coarse, guess_at, start, rounded, full, halo, rows, row_src,
+    rate_src, group_rates, tot_src, z_rates, pre_src, pre_dst,
     group_gain, z_gain, off_src, offs, sum_src, sums, back_src, back,
-    load, rate_send, rate_recv, tot_send, tot_recv, full_send, full_recv, halo_send, halo_recv,
+    load, ready, rate_send, rate_recv, tot_send, tot_recv, pre_send, pre_recv, full_send, full_recv, halo_send, halo_recv,
     row_send, row_recv, off_send, off_recv, sum_send, sum_recv, back_send, back_recv,
 ):
     cells = init_ref.shape[1]
@@ -60,9 +61,10 @@
         pltpu.make_async_copy(ref, ref, sem).wait()
 
     barrier = pltpu.get_barrier_semaphore()
-    lax.fori_loop(0, z, lambda k, c: (greet(z_peer(k)), c)[1], 0)
+    last_near = jnp.minimum(z + NEAR, depth - 1)
     others(group, j, lambda q: greet(group_peer(q)))
     others(shards, mine, lambda p: greet(space_peer(p)))
+    later(lambda k: greet(z_peer(k)))
 
     loads = [
         pltpu.make_async_copy(src, dst, load.at[n])
@@ -107,7 +109,7 @@
     own_column = column(row)
     coarse[...] = jnp.exp(-(own_column * own_scale))
 
-    pl.semaphore_wait(barrier, group + shards + depth - 3 - z)
+    pl.semaphore_wait(barrier, group + shards - 2 + z)
 
     def rate_copy(q):
         return pltpu.make_async_remote_copy(
@@ -130,6 +132,10 @@
             device_id=space_peer(p), device_id_type=MESH)
 
     others(group, j, lambda q: rate_copy(q).start())
+    lax.fori_loop(
+        0, z,
+        lambda k, c: (
+            pl.semaphore_signal(ready.at[z], inc=1, device_id=z_peer(z - 1 - k), device_id_type=MESH), c)[1], 0)
     others(shards, mine, lambda p: row_copy(p).start())
     others(shards, mine, lambda p: full_copy(p).start())
     arrived(group_rates.at[pl.ds(0, group - 1)], rate_recv)
@@ -145,7 +151,12 @@
             src_ref=tot_src, dst_ref=z_rates.at[slot], send_sem=tot_send.at[k], recv_sem=tot_recv.at[slot],
             device_id=z_peer(k), device_id_type=MESH)
 
-    later(lambda k: tot_copy(k, z).start())
+    def tell(k, carry):
+        pl.semaphore_wait(ready.at[k], 1)
+        tot_copy(k, z).start()
+        return carry
+
+    lax.fori_loop(z + 1, jnp.minimum(z + 2, depth), tell, 0)
 
     for q in range(group):
         group_gain[q] = jnp.exp(-(octet_column(group_rates[q]) * half_scale))
@@ -154,15 +165,36 @@
         decay[p] = jnp.exp(-(own_column * rows[p, 1:2, :]) / FINE)
     arrived(full.at[pl.ds(0, shards - 1)], full_recv)
 
+    def pre_copy():
+        return pltpu.make_async_remote_copy(
+            src_ref=pre_src, dst_ref=pre_dst, send_sem=pre_send, recv_sem=pre_recv,
+            device_id=z_peer(last_near), device_id_type=MESH)
+
+    lax.fori_loop(z + 2, last_near + 1, tell, 0)
+
+    pre_src[...] = jnp.zeros((1, 128), jnp.float32)
+
+    @pl.when(z >= NEAR)
+    def _():
+        pre_copy().wait_recv()
+        pre_src[...] = pre_dst[...]
+
     def add_total(k, carried):
         tot_copy(k, k).wait_recv()
         return carried + z_rates[k]
 
-    passed = column(lax.fori_loop(0, z, add_total, before))
+    ahead_of = lax.fori_loop(jnp.maximum(z - NEAR + 1, 0), z, add_total, pre_src[...])
+    pre_src[...] = ahead_of + total
+
+    @pl.when(z + NEAR < depth)
+    def _():
+        pre_copy().start()
+
+    passed = column(ahead_of + before)
     for p in range(shards):
         state[p] = jnp.exp(-(passed * rows[p, 1:2, :])) * full[p]
     guess = state[pl.ds(mine, 1)][0]
-    guess_ref[...] = guess
+    guess_at[...] = guess
     start[...] = guess
 
     lane_t = lax.broadcasted_iota(jnp.int32, (2 * DOF, LAYER), 1)
@@ -209,6 +241,14 @@
         others(group, j, lambda q: off_copy(q).start())
         offs[it, pl.ds(j, 1)] = off_src[it, pl.ds(j, 1)]
         if it == 0:
+            lax.fori_loop(last_near + 1, depth, tell, 0)
+
+            def hear(k, carry):
+                tot_copy(k, k).wait_recv()
+                return carry
+
+            lax.fori_loop(0, jnp.maximum(z - NEAR + 1, 0), hear, 0)
+
             def fill_gain(k, carry):
                 z_gain[k] = jnp.exp(-(octet_column(z_rates[k]) * half_scale))
                 return carry
@@ -247,7 +287,7 @@
         correction = jnp.concatenate(
             [jnp.concatenate([back[it, 2 * m], back[it, 2 * m + 1]], axis=1) for m in range(DOF // OCTET)], axis=0
         )
-        following = guess_ref[...] + correction
+        following = guess_at[...] + correction
         if it + 1 < ITERS:
             start[...] = following
             halo[it, pl.ds(mine, 1)] = following.astype(jnp.bfloat16)[None]
@@ -257,7 +297,9 @@
                 state[p] = halo[it, p].astype(jnp.float32)
             state[pl.ds(mine, 1)] = following[None]
         else:
-            end_ref[...] = coarse[...] * following + offset
+            end = 0.5 * (coarse[...] * following + offset)
+            sum_ref[...] = end + 0.5 * guess_at[...]
+            difference_ref[...] = end - 0.5 * guess_at[...]
 
     def left(ref, sem):
         pltpu.make_async_copy(ref, ref, sem).wait()
@@ -266,6 +308,11 @@
     left(rows.at[pl.ds(0, shards - 1)], row_send)
     left(full.at[pl.ds(0, shards - 1)], full_send)
     later(lambda k: tot_copy(k, z).wait_send())
+
+    @pl.when(z + NEAR < depth)
+    def _():
+        pre_copy().wait_send()
+
     for it in range(ITERS):
         left(off_src.at[it, pl.ds(0, group - 1)], off_send.at[it])
         left(back_src.at[it, pl.ds(0, group - 1)], back_send.at[it])
@@ -285,9 +332,9 @@
     vmem = pl.BlockSpec(memory_space=pltpu.VMEM)
     hbm = pl.BlockSpec(memory_space=pltpu.HBM)
     dma = pltpu.SemaphoreType.DMA
-    end, guess = pl.pallas_call(
+    half_sum, half_difference = pl.pallas_call(
         functools.partial(kernel, depth, group, shards),
-        out_shape=[jax.ShapeDtypeStruct((DOF, cells), f32)] * 2,
+        out_shape=[pltpu.VMEM((DOF, cells), f32)] * 2,
         in_specs=[hbm] * 6,
         out_specs=[vmem] * 2,
         scratch_shapes=[
@@ -302,6 +349,7 @@
             pltpu.VMEM((shards, DOF, cells), f32),
             pltpu.VMEM((DOF, cells), f32),
             pltpu.VMEM((DOF, cells), f32),
+            pltpu.VMEM((DOF, cells), f32),
             pltpu.VMEM((shards + 2, DOF, cells), bf16),
             pltpu.VMEM((shards, DOF, cells), f32),
             pltpu.VMEM((ITERS - 1, shards, DOF, cells), bf16),
@@ -311,6 +359,8 @@
             pltpu.VMEM((group, 1, 128), f32),
             pltpu.VMEM((1, 128), f32),
             pltpu.VMEM((depth, 1, 128), f32),
+            pltpu.VMEM((1, 128), f32),
+            pltpu.VMEM((1, 128), f32),
             pltpu.VMEM((group, OCTET, LAYER), f32),
             pltpu.VMEM((depth, OCTET, LAYER), f32),
             pltpu.VMEM((ITERS, group, OCTET, LAYER), f32),
@@ -319,7 +369,7 @@
             pltpu.VMEM((ITERS, depth, OCTET, LAYER), f32),
             pltpu.VMEM((ITERS, group, OCTET, LAYER), f32),
             pltpu.VMEM((ITERS, group, OCTET, LAYER), f32),
-            dma((6,)), dma, dma, dma((depth,)), dma((depth,)),
+            dma((6,)), pltpu.SemaphoreType.REGULAR((depth,)), dma, dma, dma((depth,)), dma((depth,)), dma, dma,
             dma, dma, dma((ITERS,)), dma((ITERS,)),
             dma, dma, dma((ITERS,)), dma((ITERS,)),
             dma((ITERS, depth)), dma((ITERS, depth)), dma((ITERS,)), dma((ITERS,)),
@@ -327,7 +377,7 @@
         compiler_params=pltpu.CompilerParams(collective_id=1, has_side_effects=True),
         name="parareal",
     )(initial_state, inv_mass[None], element_scale[None], mode_rate, volume_block, face_blocks)
-    return end[None], guess[None]
+    return (half_sum + half_difference)[None], (half_sum - half_difference)[None]
 
 
 def solution(mesh):

time: 60.6 us -> 53.8 us (0.89)
  Pallas kernels: 57.3 us -> 52 us
  local copies, waits for them, and re-layouts: 2.14 us -> 0 us
  other arithmetic: 0 us -> 0.66 us
    pallas_call x1, Pallas kernels: 57.3 us -> 52 us  [per_device(): pl.pallas_call(functools.partial(kernel, depth, group, shards), out_shape...]
    unnamed x4 -> x0, local copies, waits for them, and re-layouts: 2.14 us -> none
    broadcast_in_dim x0 -> x1, other arithmetic: none -> 0.66 us  [per_device(): (half_sum - half_difference)[None]]
where the time goes in v3:
time: 53.8 us; the launch traced here: 53.3 us
  Pallas kernels  52 us (97%)
  other arithmetic  0.66 us (1%)
  between operations  0.64 us (1%)
    pallas_call x1, Pallas kernels, per_device(): pl.pallas_call(functools.partial(kernel, depth, group, shards), out_shape...  52 us

profile of v3, /device:TPU:480, one launch (start us, length us, event | category | flops | bytes accessed | tf_op | source)
XLA Modules:
  0.0 53.3 jit_solution(11346942915652504611)
XLA Ops:
  0.6 52.0 %parareal.1 = (f32[64,256]{1,0:T(8,128)S(1)}, f32[64,256]{1,0:T(8,128)S(1)}) custom-call(f32[64,256]{1,0:T(8,128)} %init_hbm.1, f32[1,256]{1,0:T(1,128)} %bitcast.6, f32[1,256]{1,0:T(1,128)} %bitcast.7, f32[1,64]{1,0:T(1,128)} %rate_hbm.1, bf16[64,64]{1,0:T(8,128)(2,1)} %volume_hbm.1, bf16[6,64,64]{2,1,0:T(8,128)(2,1)} %faces_hbm.1), custom_call_target="tpu_custom_call" | custom-call | tf_op jit(solution)/shard_map/parareal/pallas_call | solution.py:335
  52.6 0.7 %subtract_bitcast_fusion = (f32[1,64,256]{2,1,0:T(8,128)}, f32[1,64,256]{2,1,0:T(8,128)}) fusion(f32[64,256]{1,0:T(8,128)S(1)} %get-tuple-element.4, f32[64,256]{1,0:T(8,128)S(1)} %get-tuple-element.5), kind=kLoop, calls=%fused_computation | loop fusion | flops 32768 | bytes 262144 | tf_op jit(solution)/shard_map/broadcast_in_dim | solution.py:380

commit v4 on v3

--- a/solution.py
+++ b/solution.py
@@ -14,7 +14,7 @@
 ITERS = 2
 LAYER = EY * EZ
 OCTET = 8
-NEAR = 2
+NEAR = 4
 MESH = pl.DeviceIdType.MESH
 
 
@@ -23,11 +23,11 @@
     init_hbm, mass_hbm, scale_hbm, rate_hbm, volume_hbm, faces_hbm,
     sum_ref, difference_ref,
     init_ref, mass_ref, scale_ref, rate_ref, volume_ref, faces_ref,
-    blocks, state, decay, coarse, guess_at, start, rounded, full, halo, rows, row_src,
+    blocks, state, decay, coarse, guess_at, start, rounded, full, plane_guess, halo_src, halo, rows, row_src,
     rate_src, group_rates, tot_src, z_rates, pre_src, pre_dst,
-    group_gain, z_gain, off_src, offs, sum_src, sums, back_src, back,
+    group_gain, z_gain, off_src, offs, sum_src, sums, run_src, run_dst, back_src, back,
     load, ready, rate_send, rate_recv, tot_send, tot_recv, pre_send, pre_recv, full_send, full_recv, halo_send, halo_recv,
-    row_send, row_recv, off_send, off_recv, sum_send, sum_recv, back_send, back_recv,
+    row_send, row_recv, off_send, off_recv, sum_send, sum_recv, run_send, run_recv, back_send, back_recv,
 ):
     cells = init_ref.shape[1]
     time = lax.axis_index("tm")
@@ -51,8 +51,8 @@
 
         lax.fori_loop(0, count - 1, step, 0)
 
-    def later(body):
-        lax.fori_loop(0, depth - 1 - z, lambda d, c: (body(depth - 1 - d), c)[1], 0)
+    def nearest(body):
+        lax.fori_loop(z + 1, jnp.minimum(z + NEAR, depth), lambda k, c: (body(k), c)[1], 0)
 
     def greet(peer):
         pl.semaphore_signal(barrier, inc=1, device_id=peer, device_id_type=MESH)
@@ -61,10 +61,10 @@
         pltpu.make_async_copy(ref, ref, sem).wait()
 
     barrier = pltpu.get_barrier_semaphore()
-    last_near = jnp.minimum(z + NEAR, depth - 1)
+    first_near = jnp.maximum(z - NEAR + 1, 0)
     others(group, j, lambda q: greet(group_peer(q)))
     others(shards, mine, lambda p: greet(space_peer(p)))
-    later(lambda k: greet(z_peer(k)))
+    lax.fori_loop(z + 1, jnp.minimum(z + NEAR + 1, depth), lambda k, c: (greet(z_peer(k)), c)[1], 0)
 
     loads = [
         pltpu.make_async_copy(src, dst, load.at[n])
@@ -83,7 +83,7 @@
     lane = lax.broadcasted_iota(jnp.int32, (DOF, 128), 1)
     sub_o = lax.broadcasted_iota(jnp.int32, (OCTET, 128), 0)
     lane_o = lax.broadcasted_iota(jnp.int32, (OCTET, 128), 1)
-    first_mode = OCTET * (j // 2)
+    first_mode = OCTET * j
 
     def column(values):
         return jnp.sum(jnp.where(sub == lane, values, 0.0), axis=1, keepdims=True)
@@ -105,11 +105,10 @@
     for f in range(6):
         blocks[:, DOF * (f + 1) : DOF * (f + 2)] = faces_ref[f]
     own_scale = scale_ref[...]
-    half_scale = scale_ref[:, pl.ds(pl.multiple_of(LAYER * lax.rem(j, 2), LAYER), LAYER)]
     own_column = column(row)
     coarse[...] = jnp.exp(-(own_column * own_scale))
 
-    pl.semaphore_wait(barrier, group + shards - 2 + z)
+    pl.semaphore_wait(barrier, group + shards - 2 + jnp.minimum(z, NEAR))
 
     def rate_copy(q):
         return pltpu.make_async_remote_copy(
@@ -121,10 +120,10 @@
             src_ref=init_ref, dst_ref=full.at[mine], send_sem=full_send, recv_sem=full_recv,
             device_id=space_peer(p), device_id_type=MESH)
 
-    def halo_copy(it, p):
-        return pltpu.make_async_remote_copy(
-            src_ref=halo.at[it, mine], dst_ref=halo.at[it, mine], send_sem=halo_send.at[it],
-            recv_sem=halo_recv.at[it], device_id=space_peer(p), device_id_type=MESH)
+    def halo_copy(it, q, p):
+        return pltpu.make_async_remote_copy(
+            src_ref=halo_src.at[it, q], dst_ref=halo.at[it, mine, j], send_sem=halo_send.at[it],
+            recv_sem=halo_recv.at[it], device_id=(z * group + q, p), device_id_type=MESH)
 
     def row_copy(p):
         return pltpu.make_async_remote_copy(
@@ -133,7 +132,7 @@
 
     others(group, j, lambda q: rate_copy(q).start())
     lax.fori_loop(
-        0, z,
+        0, jnp.minimum(z, NEAR),
         lambda k, c: (
             pl.semaphore_signal(ready.at[z], inc=1, device_id=z_peer(z - 1 - k), device_id_type=MESH), c)[1], 0)
     others(shards, mine, lambda p: row_copy(p).start())
@@ -159,7 +158,7 @@
     lax.fori_loop(z + 1, jnp.minimum(z + 2, depth), tell, 0)
 
     for q in range(group):
-        group_gain[q] = jnp.exp(-(octet_column(group_rates[q]) * half_scale))
+        group_gain[q] = jnp.exp(-(octet_column(group_rates[q]) * own_scale))
     arrived(rows.at[pl.ds(0, shards - 1)], row_recv)
     for p in range(shards):
         decay[p] = jnp.exp(-(own_column * rows[p, 1:2, :]) / FINE)
@@ -168,9 +167,9 @@
     def pre_copy():
         return pltpu.make_async_remote_copy(
             src_ref=pre_src, dst_ref=pre_dst, send_sem=pre_send, recv_sem=pre_recv,
-            device_id=z_peer(last_near), device_id_type=MESH)
-
-    lax.fori_loop(z + 2, last_near + 1, tell, 0)
+            device_id=z_peer(z + NEAR), device_id_type=MESH)
+
+    lax.fori_loop(z + 2, jnp.minimum(z + NEAR, depth), tell, 0)
 
     pre_src[...] = jnp.zeros((1, 128), jnp.float32)
 
@@ -183,11 +182,12 @@
         tot_copy(k, k).wait_recv()
         return carried + z_rates[k]
 
-    ahead_of = lax.fori_loop(jnp.maximum(z - NEAR + 1, 0), z, add_total, pre_src[...])
+    ahead_of = lax.fori_loop(first_near, z, add_total, pre_src[...])
     pre_src[...] = ahead_of + total
 
     @pl.when(z + NEAR < depth)
     def _():
+        pl.semaphore_wait(ready.at[z + NEAR], 1)
         pre_copy().start()
 
     passed = column(ahead_of + before)
@@ -230,8 +230,7 @@
     for it in range(ITERS):
         lax.fori_loop(0, FINE, fine_step, 0, unroll=FINE)
         offset = state[pl.ds(mine, 1)][0] - coarse[...] * start[...]
-        for q in range(group):
-            off_src[it, q] = offset[OCTET * (q // 2) : OCTET * (q // 2 + 1), LAYER * (q % 2) : LAYER * (q % 2 + 1)]
+        off_src[it] = offset.reshape(group, OCTET, cells)
 
         def off_copy(q):
             return pltpu.make_async_remote_copy(
@@ -241,19 +240,16 @@
         others(group, j, lambda q: off_copy(q).start())
         offs[it, pl.ds(j, 1)] = off_src[it, pl.ds(j, 1)]
         if it == 0:
-            lax.fori_loop(last_near + 1, depth, tell, 0)
-
-            def hear(k, carry):
-                tot_copy(k, k).wait_recv()
+            def fill_gain(k, carry):
+                z_gain[k] = jnp.exp(-(octet_column(z_rates[k]) * own_scale))
                 return carry
 
-            lax.fori_loop(0, jnp.maximum(z - NEAR + 1, 0), hear, 0)
-
-            def fill_gain(k, carry):
-                z_gain[k] = jnp.exp(-(octet_column(z_rates[k]) * half_scale))
-                return carry
-
-            lax.fori_loop(0, z, fill_gain, 0)
+            lax.fori_loop(first_near, z, fill_gain, 0)
+            own_init = init_ref[pl.ds(pl.multiple_of(first_mode, OCTET), OCTET), :]
+            since = ahead_of
+            for q in range(group):
+                plane_guess[q] = jnp.exp(-(octet_column(since) * own_scale)) * own_init
+                since = since + group_rates[q]
         arrived(offs.at[it, pl.ds(0, group - 1)], off_recv.at[it])
         part = offs[it, 0]
         for q in range(1, group):
@@ -265,16 +261,33 @@
                 src_ref=sum_src.at[it], dst_ref=sums.at[it, slot], send_sem=sum_send.at[it, k],
                 recv_sem=sum_recv.at[it, slot], device_id=z_peer(k), device_id_type=MESH)
 
-        later(lambda k: sum_copy(k, z).start())
+        nearest(lambda k: sum_copy(k, z).start())
+
+        def run_copy():
+            return pltpu.make_async_remote_copy(
+                src_ref=run_src.at[it], dst_ref=run_dst.at[it], send_sem=run_send.at[it],
+                recv_sem=run_recv.at[it], device_id=z_peer(z + NEAR), device_id_type=MESH)
+
+        run_src[it] = jnp.zeros((OCTET, cells), jnp.float32)
+
+        @pl.when(z >= NEAR)
+        def _():
+            run_copy().wait_recv()
+            run_src[it] = run_dst[it]
 
         def add_sum(k, carried):
             sum_copy(k, k).wait_recv()
             return z_gain[k] * carried + sums[it, k]
 
-        carried = lax.fori_loop(0, z, add_sum, jnp.zeros((OCTET, LAYER), jnp.float32))
+        carried = lax.fori_loop(first_near, z, add_sum, run_src[it])
         for q in range(group):
             back_src[it, q] = carried
             carried = group_gain[q] * carried + offs[it, q]
+        run_src[it] = carried
+
+        @pl.when(z + NEAR < depth)
+        def _():
+            run_copy().start()
 
         def back_copy(q):
             return pltpu.make_async_remote_copy(
@@ -282,19 +295,28 @@
                 recv_sem=back_recv.at[it], device_id=group_peer(q), device_id_type=MESH)
 
         others(group, j, lambda q: back_copy(q).start())
+        if it + 1 < ITERS:
+            for q in range(group):
+                piece = plane_guess[q] + back_src[it, q]
+                piece = jnp.concatenate([piece[:, n * LAYER : (n + 1) * LAYER] for n in range(2)], axis=0)
+                halo_src[it, q] = piece.astype(jnp.bfloat16)
+
+            def fan(p):
+                others(group, j, lambda q: halo_copy(it, q, p).start())
+                halo_copy(it, j, p).start()
+
+            others(shards, mine, fan)
         back[it, pl.ds(j, 1)] = back_src[it, pl.ds(j, 1)]
         arrived(back.at[it, pl.ds(0, group - 1)], back_recv.at[it])
-        correction = jnp.concatenate(
-            [jnp.concatenate([back[it, 2 * m], back[it, 2 * m + 1]], axis=1) for m in range(DOF // OCTET)], axis=0
-        )
+        correction = back[it].reshape(DOF, cells)
         following = guess_at[...] + correction
         if it + 1 < ITERS:
             start[...] = following
-            halo[it, pl.ds(mine, 1)] = following.astype(jnp.bfloat16)[None]
-            others(shards, mine, lambda p: halo_copy(it, p).start())
             arrived(halo.at[it, pl.ds(0, shards - 1)], halo_recv.at[it])
             for p in range(shards):
-                state[p] = halo[it, p].astype(jnp.float32)
+                for q in range(group):
+                    piece = halo[it, p, q].astype(jnp.float32)
+                    state[p, q * OCTET : (q + 1) * OCTET, :] = jnp.concatenate([piece[:OCTET], piece[OCTET:]], axis=1)
             state[pl.ds(mine, 1)] = following[None]
         else:
             end = 0.5 * (coarse[...] * following + offset)
@@ -307,7 +329,7 @@
     left(group_rates.at[pl.ds(0, group - 1)], rate_send)
     left(rows.at[pl.ds(0, shards - 1)], row_send)
     left(full.at[pl.ds(0, shards - 1)], full_send)
-    later(lambda k: tot_copy(k, z).wait_send())
+    nearest(lambda k: tot_copy(k, z).wait_send())
 
     @pl.when(z + NEAR < depth)
     def _():
@@ -322,7 +344,11 @@
         def summed(k):
             pltpu.make_async_copy(sum_src.at[it], sum_src.at[it], sum_send.at[it, k]).wait()
 
-        later(summed)
+        nearest(summed)
+
+        @pl.when(z + NEAR < depth)
+        def _():
+            pltpu.make_async_copy(run_src.at[it], run_src.at[it], run_send.at[it]).wait()
 
 
 def per_device(depth, group, initial_state, inv_mass, element_scale, mode_rate, volume_block, face_blocks):
@@ -352,7 +378,9 @@
             pltpu.VMEM((DOF, cells), f32),
             pltpu.VMEM((shards + 2, DOF, cells), bf16),
             pltpu.VMEM((shards, DOF, cells), f32),
-            pltpu.VMEM((ITERS - 1, shards, DOF, cells), bf16),
+            pltpu.VMEM((group, OCTET, cells), f32),
+            pltpu.VMEM((ITERS - 1, group, 2 * OCTET, LAYER), bf16),
+            pltpu.VMEM((ITERS - 1, shards, group, 2 * OCTET, LAYER), bf16),
             pltpu.VMEM((shards, 8, cells), f32),
             pltpu.VMEM((8, cells), f32),
             pltpu.VMEM((1, 128), f32),
@@ -361,18 +389,20 @@
             pltpu.VMEM((depth, 1, 128), f32),
             pltpu.VMEM((1, 128), f32),
             pltpu.VMEM((1, 128), f32),
-            pltpu.VMEM((group, OCTET, LAYER), f32),
-            pltpu.VMEM((depth, OCTET, LAYER), f32),
-            pltpu.VMEM((ITERS, group, OCTET, LAYER), f32),
-            pltpu.VMEM((ITERS, group, OCTET, LAYER), f32),
-            pltpu.VMEM((ITERS, OCTET, LAYER), f32),
-            pltpu.VMEM((ITERS, depth, OCTET, LAYER), f32),
-            pltpu.VMEM((ITERS, group, OCTET, LAYER), f32),
-            pltpu.VMEM((ITERS, group, OCTET, LAYER), f32),
+            pltpu.VMEM((group, OCTET, cells), f32),
+            pltpu.VMEM((depth, OCTET, cells), f32),
+            pltpu.VMEM((ITERS, group, OCTET, cells), f32),
+            pltpu.VMEM((ITERS, group, OCTET, cells), f32),
+            pltpu.VMEM((ITERS, OCTET, cells), f32),
+            pltpu.VMEM((ITERS, depth, OCTET, cells), f32),
+            pltpu.VMEM((ITERS, OCTET, cells), f32),
+            pltpu.VMEM((ITERS, OCTET, cells), f32),
+            pltpu.VMEM((ITERS, group, OCTET, cells), f32),
+            pltpu.VMEM((ITERS, group, OCTET, cells), f32),
             dma((6,)), pltpu.SemaphoreType.REGULAR((depth,)), dma, dma, dma((depth,)), dma((depth,)), dma, dma,
             dma, dma, dma((ITERS,)), dma((ITERS,)),
             dma, dma, dma((ITERS,)), dma((ITERS,)),
-            dma((ITERS, depth)), dma((ITERS, depth)), dma((ITERS,)), dma((ITERS,)),
+            dma((ITERS, depth)), dma((ITERS, depth)), dma((ITERS,)), dma((ITERS,)), dma((ITERS,)), dma((ITERS,)),
         ],
         compiler_params=pltpu.CompilerParams(collective_id=1, has_side_effects=True),
         name="parareal",
@@ -382,7 +412,7 @@
 
 def solution(mesh):
     slices = mesh.shape["tm"]
-    group = (DOF // OCTET) * 2
+    group = DOF // OCTET
     placed = (P(None, "space"), P("space"), P("space"), P("tm", None), P(), P())
     return jax.shard_map(
         functools.partial(per_device, slices // group, group),

time: 53.8 us -> 50.7 us (0.942)
  Pallas kernels: 52 us -> 49.3 us
    pallas_call x1, Pallas kernels: 52 us -> 49.3 us  [per_device(): pl.pallas_call(functools.partial(kernel, depth, group, shards), out_shape...]
where the time goes in v4:
time: 50.7 us; the launch traced here: 50.6 us
  Pallas kernels  49.3 us (97%)
  other arithmetic  0.66 us (1%)
  between operations  0.64 us (1%)
    pallas_call x1, Pallas kernels, per_device(): pl.pallas_call(functools.partial(kernel, depth, group, shards), out_shape...  49.3 us

profile of v4, /device:TPU:480, one launch (start us, length us, event | category | flops | bytes accessed | tf_op | source)
XLA Modules:
  0.0 50.6 jit_solution(16545394280061396631)
XLA Ops:
  0.6 49.3 %parareal.1 = (f32[64,256]{1,0:T(8,128)S(1)}, f32[64,256]{1,0:T(8,128)S(1)}) custom-call(f32[64,256]{1,0:T(8,128)} %init_hbm.1, f32[1,256]{1,0:T(1,128)} %bitcast.6, f32[1,256]{1,0:T(1,128)} %bitcast.7, f32[1,64]{1,0:T(1,128)} %rate_hbm.1, bf16[64,64]{1,0:T(8,128)(2,1)} %volume_hbm.1, bf16[6,64,64]{2,1,0:T(8,128)(2,1)} %faces_hbm.1), custom_call_target="tpu_custom_call" | custom-call | tf_op jit(solution)/shard_map/parareal/pallas_call | solution.py:361
  49.9 0.7 %subtract_bitcast_fusion = (f32[1,64,256]{2,1,0:T(8,128)}, f32[1,64,256]{2,1,0:T(8,128)}) fusion(f32[64,256]{1,0:T(8,128)S(1)} %get-tuple-element.4, f32[64,256]{1,0:T(8,128)S(1)} %get-tuple-element.5), kind=kLoop, calls=%fused_computation | loop fusion | flops 32768 | bytes 262144 | tf_op jit(solution)/shard_map/broadcast_in_dim | solution.py:410

commit v5 on v4

--- a/solution.py
+++ b/solution.py
@@ -49,7 +49,7 @@
             body(lax.rem(me + 1 + d, count))
             return carry
 
-        lax.fori_loop(0, count - 1, step, 0)
+        lax.fori_loop(0, count - 1, step, 0, unroll=True)
 
     def nearest(body):
         lax.fori_loop(z + 1, jnp.minimum(z + NEAR, depth), lambda k, c: (body(k), c)[1], 0)
@@ -226,6 +226,35 @@
             state[p] = decay[p] * state[p] + rows[p, 0:1, :] * change
         return carry
 
+    def leave():
+        def left(ref, sem):
+            pltpu.make_async_copy(ref, ref, sem).wait()
+
+        left(group_rates.at[pl.ds(0, group - 1)], rate_send)
+        left(rows.at[pl.ds(0, shards - 1)], row_send)
+        left(full.at[pl.ds(0, shards - 1)], full_send)
+        nearest(lambda k: tot_copy(k, z).wait_send())
+
+        @pl.when(z + NEAR < depth)
+        def _():
+            pre_copy().wait_send()
+
+        for it in range(ITERS):
+            left(off_src.at[it, pl.ds(0, group - 1)], off_send.at[it])
+            if it + 1 < ITERS:
+                left(back_src.at[it, pl.ds(0, group - 1)], back_send.at[it])
+            if it + 1 < ITERS:
+                left(halo.at[it, pl.ds(0, shards - 1)], halo_send.at[it])
+
+            def summed(k):
+                pltpu.make_async_copy(sum_src.at[it], sum_src.at[it], sum_send.at[it, k]).wait()
+
+            nearest(summed)
+
+            @pl.when(z + NEAR < depth)
+            def _():
+                pltpu.make_async_copy(run_src.at[it], run_src.at[it], run_send.at[it]).wait()
+
     offset = None
     for it in range(ITERS):
         lax.fori_loop(0, FINE, fine_step, 0, unroll=FINE)
@@ -294,7 +323,6 @@
                 src_ref=back_src.at[it, q], dst_ref=back.at[it, j], send_sem=back_send.at[it],
                 recv_sem=back_recv.at[it], device_id=group_peer(q), device_id_type=MESH)
 
-        others(group, j, lambda q: back_copy(q).start())
         if it + 1 < ITERS:
             for q in range(group):
                 piece = plane_guess[q] + back_src[it, q]
@@ -306,7 +334,11 @@
                 halo_copy(it, j, p).start()
 
             others(shards, mine, fan)
+
+        others(group, j, lambda q: back_copy(q).start())
         back[it, pl.ds(j, 1)] = back_src[it, pl.ds(j, 1)]
+        if it + 1 == ITERS:
+            leave()
         arrived(back.at[it, pl.ds(0, group - 1)], back_recv.at[it])
         correction = back[it].reshape(DOF, cells)
         following = guess_at[...] + correction
@@ -322,33 +354,7 @@
             end = 0.5 * (coarse[...] * following + offset)
             sum_ref[...] = end + 0.5 * guess_at[...]
             difference_ref[...] = end - 0.5 * guess_at[...]
-
-    def left(ref, sem):
-        pltpu.make_async_copy(ref, ref, sem).wait()
-
-    left(group_rates.at[pl.ds(0, group - 1)], rate_send)
-    left(rows.at[pl.ds(0, shards - 1)], row_send)
-    left(full.at[pl.ds(0, shards - 1)], full_send)
-    nearest(lambda k: tot_copy(k, z).wait_send())
-
-    @pl.when(z + NEAR < depth)
-    def _():
-        pre_copy().wait_send()
-
-    for it in range(ITERS):
-        left(off_src.at[it, pl.ds(0, group - 1)], off_send.at[it])
-        left(back_src.at[it, pl.ds(0, group - 1)], back_send.at[it])
-        if it + 1 < ITERS:
-            left(halo.at[it, pl.ds(0, shards - 1)], halo_send.at[it])
-
-        def summed(k):
-            pltpu.make_async_copy(sum_src.at[it], sum_src.at[it], sum_send.at[it, k]).wait()
-
-        nearest(summed)
-
-        @pl.when(z + NEAR < depth)
-        def _():
-            pltpu.make_async_copy(run_src.at[it], run_src.at[it], run_send.at[it]).wait()
+            arrived(back_src.at[it, pl.ds(0, group - 1)], back_send.at[it])
 
 
 def per_device(depth, group, initial_state, inv_mass, element_scale, mode_rate, volume_block, face_blocks):

time: 50.7 us -> 50.6 us (level)
  no operation moved by 1% of the time
where the time goes in v5:
time: 50.6 us; the launch traced here: 50.4 us
  Pallas kernels  49.1 us (97%)
  other arithmetic  0.66 us (1%)
  between operations  0.64 us (1%)
    pallas_call x1, Pallas kernels, per_device(): pl.pallas_call(functools.partial(kernel, depth, group, shards), out_shape...  49.1 us

profile of v5, /device:TPU:480, one launch (start us, length us, event | category | flops | bytes accessed | tf_op | source)
XLA Modules:
  0.0 50.4 jit_solution(8713242428282980109)
XLA Ops:
  0.6 49.1 %parareal.1 = (f32[64,256]{1,0:T(8,128)S(1)}, f32[64,256]{1,0:T(8,128)S(1)}) custom-call(f32[64,256]{1,0:T(8,128)} %init_hbm.1, f32[1,256]{1,0:T(1,128)} %bitcast.6, f32[1,256]{1,0:T(1,128)} %bitcast.7, f32[1,64]{1,0:T(1,128)} %rate_hbm.1, bf16[64,64]{1,0:T(8,128)(2,1)} %volume_hbm.1, bf16[6,64,64]{2,1,0:T(8,128)(2,1)} %faces_hbm.1), custom_call_target="tpu_custom_call" | custom-call | tf_op jit(solution)/shard_map/parareal/pallas_call | solution.py:367
  49.7 0.7 %subtract_bitcast_fusion = (f32[1,64,256]{2,1,0:T(8,128)}, f32[1,64,256]{2,1,0:T(8,128)}) fusion(f32[64,256]{1,0:T(8,128)S(1)} %get-tuple-element.4, f32[64,256]{1,0:T(8,128)S(1)} %get-tuple-element.5), kind=kLoop, calls=%fused_computation | loop fusion | flops 32768 | bytes 262144 | tf_op jit(solution)/shard_map/broadcast_in_dim | solution.py:416

commit v6 on v5

--- a/solution.py
+++ b/solution.py
@@ -23,7 +23,7 @@
     init_hbm, mass_hbm, scale_hbm, rate_hbm, volume_hbm, faces_hbm,
     sum_ref, difference_ref,
     init_ref, mass_ref, scale_ref, rate_ref, volume_ref, faces_ref,
-    blocks, state, decay, coarse, guess_at, start, rounded, full, plane_guess, halo_src, halo, rows, row_src,
+    blocks, state, decay, mass, coarse, guess_at, start, full, plane_guess, halo_src, halo, rows, row_src,
     rate_src, group_rates, tot_src, z_rates, pre_src, pre_dst,
     group_gain, z_gain, off_src, offs, sum_src, sums, run_src, run_dst, back_src, back,
     load, ready, rate_send, rate_recv, tot_send, tot_recv, pre_send, pre_recv, full_send, full_recv, halo_send, halo_recv,
@@ -76,9 +76,6 @@
     for copy in loads:
         copy.start()
 
-    zero_part = jnp.zeros((DOF, cells), jnp.bfloat16)
-    rounded[0] = zero_part
-    rounded[shards + 1] = zero_part
     sub = lax.broadcasted_iota(jnp.int32, (DOF, 128), 0)
     lane = lax.broadcasted_iota(jnp.int32, (DOF, 128), 1)
     sub_o = lax.broadcasted_iota(jnp.int32, (OCTET, 128), 0)
@@ -101,9 +98,23 @@
     )
     rows[pl.ds(mine, 1)] = row_src[...][None]
     full[pl.ds(mine, 1)] = init_ref[...][None]
-    blocks[:, :DOF] = volume_ref[...]
-    for f in range(6):
-        blocks[:, DOF * (f + 1) : DOF * (f + 2)] = faces_ref[f]
+    turned = [volume_ref[...]] + [faces_ref[f] for f in range(6)]
+    turned = [block.astype(jnp.float32).T.astype(jnp.bfloat16) for block in turned]
+    none = jnp.zeros((DOF, DOF), jnp.bfloat16)
+    grid = [[turned[0], turned[1]], [turned[2], turned[0]], [none, turned[2]], [turned[1], none]]
+    for f in range(3, 7):
+        grid += [[turned[f], none], [none, turned[f]]]
+    for n, (left_block, right_block) in enumerate(grid):
+        blocks[DOF * n : DOF * (n + 1), :DOF] = left_block
+        blocks[DOF * n : DOF * (n + 1), DOF:] = right_block
+
+    def tall(value):
+        return jnp.concatenate([value[:, :LAYER], value[:, LAYER:]], axis=0).T
+
+    def flat(value):
+        value = value.T
+        return jnp.concatenate([value[:DOF], value[DOF:]], axis=1)
+
     own_scale = scale_ref[...]
     own_column = column(row)
     coarse[...] = jnp.exp(-(own_column * own_scale))
@@ -161,7 +172,8 @@
         group_gain[q] = jnp.exp(-(octet_column(group_rates[q]) * own_scale))
     arrived(rows.at[pl.ds(0, shards - 1)], row_recv)
     for p in range(shards):
-        decay[p] = jnp.exp(-(own_column * rows[p, 1:2, :]) / FINE)
+        decay[p] = tall(jnp.exp(-(own_column * rows[p, 1:2, :]) / FINE))
+        mass[p] = tall(jnp.broadcast_to(rows[p, 0:1, :], (DOF, cells)))
     arrived(full.at[pl.ds(0, shards - 1)], full_recv)
 
     def pre_copy():
@@ -192,38 +204,29 @@
 
     passed = column(ahead_of + before)
     for p in range(shards):
-        state[p] = jnp.exp(-(passed * rows[p, 1:2, :])) * full[p]
-    guess = state[pl.ds(mine, 1)][0]
+        state[p] = tall(jnp.exp(-(passed * rows[p, 1:2, :])) * full[p])
+    guess = jnp.exp(-(passed * own_scale)) * init_ref[...]
     guess_at[...] = guess
     start[...] = guess
 
-    lane_t = lax.broadcasted_iota(jnp.int32, (2 * DOF, LAYER), 1)
-    lane_z = lax.rem(lane_t, EZ)
-    lower_of = lane_t - lane_z + lax.rem(lane_z + EZ - 1, EZ)
-    upper_of = lane_t - lane_z + lax.rem(lane_z + 1, EZ)
+    low = lax.broadcasted_iota(jnp.int32, (LAYER, 2 * DOF), 1) < DOF
+
+    def turn(value, by):
+        return pltpu.roll(value.reshape(EY, EZ, 2 * DOF), by, 1).reshape(LAYER, 2 * DOF)
 
     def fine_step(step, carry):
+        old = [state[p] for p in range(shards)]
+        edge = jnp.zeros((LAYER, 2 * DOF), jnp.float32)
         for p in range(shards):
-            rounded[p + 1] = state[p].astype(jnp.bfloat16)
-        for p in range(shards):
-            centre = rounded[p + 1]
-            behind = jnp.concatenate([rounded[p, :, LAYER:], rounded[p + 1, :, :LAYER]], axis=1)
-            ahead = jnp.concatenate([rounded[p + 1, :, LAYER:], rounded[p + 2, :, :LAYER]], axis=1)
-            tall = jnp.concatenate([state[p, :, :LAYER], state[p, :, LAYER:]], axis=0)
-            south = pltpu.roll(tall, EZ, 1)
-            north = pltpu.roll(tall, LAYER - EZ, 1)
-            lower = jnp.take_along_axis(tall, lower_of, axis=1, mode="promise_in_bounds")
-            upper = jnp.take_along_axis(tall, upper_of, axis=1, mode="promise_in_bounds")
-
-            def wide(value):
-                value = value.astype(jnp.bfloat16)
-                return jnp.concatenate([value[:DOF], value[DOF:]], axis=1)
-
-            stacked = jnp.concatenate(
-                [centre, behind, ahead, wide(south), wide(north), wide(lower), wide(upper)], axis=0
-            )
-            change = jnp.dot(blocks[...], stacked, preferred_element_type=jnp.float32)
-            state[p] = decay[p] * state[p] + rows[p, 0:1, :] * change
+            value = old[p]
+            beside = jnp.where(low, old[p + 1] if p + 1 < shards else edge, old[p - 1] if p else edge)
+            parts = [
+                value, beside, pltpu.roll(value, EZ, 0), pltpu.roll(value, LAYER - EZ, 0),
+                turn(value, 1), turn(value, EZ - 1),
+            ]
+            stacked = jnp.concatenate([part.astype(jnp.bfloat16) for part in parts], axis=1)
+            change = jnp.dot(stacked, blocks[...], preferred_element_type=jnp.float32)
+            state[p] = decay[p] * value + mass[p] * change
         return carry
 
     def leave():
@@ -258,7 +261,7 @@
     offset = None
     for it in range(ITERS):
         lax.fori_loop(0, FINE, fine_step, 0, unroll=FINE)
-        offset = state[pl.ds(mine, 1)][0] - coarse[...] * start[...]
+        offset = flat(state[pl.ds(mine, 1)][0]) - coarse[...] * start[...]
         off_src[it] = offset.reshape(group, OCTET, cells)
 
         def off_copy(q):
@@ -346,10 +349,10 @@
             start[...] = following
             arrived(halo.at[it, pl.ds(0, shards - 1)], halo_recv.at[it])
             for p in range(shards):
-                for q in range(group):
-                    piece = halo[it, p, q].astype(jnp.float32)
-                    state[p, q * OCTET : (q + 1) * OCTET, :] = jnp.concatenate([piece[:OCTET], piece[OCTET:]], axis=1)
-            state[pl.ds(mine, 1)] = following[None]
+                pieces = [halo[it, p, q].astype(jnp.float32) for q in range(group)]
+                state[p] = jnp.concatenate(
+                    [piece[:OCTET] for piece in pieces] + [piece[OCTET:] for piece in pieces], axis=0).T
+            state[pl.ds(mine, 1)] = tall(following)[None]
         else:
             end = 0.5 * (coarse[...] * following + offset)
             sum_ref[...] = end + 0.5 * guess_at[...]
@@ -376,13 +379,13 @@
             pltpu.VMEM((1, DOF), f32),
             pltpu.VMEM((DOF, DOF), bf16),
             pltpu.VMEM((6, DOF, DOF), bf16),
-            pltpu.VMEM((DOF, 7 * DOF), bf16),
-            pltpu.VMEM((shards, DOF, cells), f32),
-            pltpu.VMEM((shards, DOF, cells), f32),
+            pltpu.VMEM((12 * DOF, 2 * DOF), bf16),
+            pltpu.VMEM((shards, LAYER, 2 * DOF), f32),
+            pltpu.VMEM((shards, LAYER, 2 * DOF), f32),
+            pltpu.VMEM((shards, LAYER, 2 * DOF), f32),
             pltpu.VMEM((DOF, cells), f32),
             pltpu.VMEM((DOF, cells), f32),
             pltpu.VMEM((DOF, cells), f32),
-            pltpu.VMEM((shards + 2, DOF, cells), bf16),
             pltpu.VMEM((shards, DOF, cells), f32),
             pltpu.VMEM((group, OCTET, cells), f32),
             pltpu.VMEM((ITERS - 1, group, 2 * OCTET, LAYER), bf16),

time: 50.6 us -> 49.4 us (0.976)
  Pallas kernels: 49.1 us -> 47.9 us
    pallas_call x1, Pallas kernels: 49.1 us -> 47.9 us  [per_device(): pl.pallas_call(functools.partial(kernel, depth, group, shards), out_shape...]
where the time goes in v6:
time: 49.4 us; the launch traced here: 49.3 us
  Pallas kernels  47.9 us (97%)
  other arithmetic  0.66 us (1%)
  between operations  0.64 us (1%)
    pallas_call x1, Pallas kernels, per_device(): pl.pallas_call(functools.partial(kernel, depth, group, shards), out_shape...  47.9 us

profile of v6, /device:TPU:480, one launch (start us, length us, event | category | flops | bytes accessed | tf_op | source)
XLA Modules:
  0.0 49.3 jit_solution(15930010791107155552)
XLA Ops:
  0.6 47.9 %parareal.1 = (f32[64,256]{1,0:T(8,128)S(1)}, f32[64,256]{1,0:T(8,128)S(1)}) custom-call(f32[64,256]{1,0:T(8,128)} %init_hbm.1, f32[1,256]{1,0:T(1,128)} %bitcast.6, f32[1,256]{1,0:T(1,128)} %bitcast.7, f32[1,64]{1,0:T(1,128)} %rate_hbm.1, bf16[64,64]{1,0:T(8,128)(2,1)} %volume_hbm.1, bf16[6,64,64]{2,1,0:T(8,128)(2,1)} %faces_hbm.1), custom_call_target="tpu_custom_call" | custom-call | tf_op jit(solution)/shard_map/parareal/pallas_call | solution.py:370
  48.6 0.7 %subtract_bitcast_fusion = (f32[1,64,256]{2,1,0:T(8,128)}, f32[1,64,256]{2,1,0:T(8,128)}) fusion(f32[64,256]{1,0:T(8,128)S(1)} %get-tuple-element.4, f32[64,256]{1,0:T(8,128)S(1)} %get-tuple-element.5), kind=kLoop, calls=%fused_computation | loop fusion | flops 32768 | bytes 262144 | tf_op jit(solution)/shard_map/broadcast_in_dim | solution.py:419

commit v7 on v6

--- a/solution.py
+++ b/solution.py
@@ -44,15 +44,25 @@
     def space_peer(p):
         return (time, p)
 
-    def others(count, me, body):
-        def step(d, carry):
-            body(lax.rem(me + 1 + d, count))
-            return carry
-
-        lax.fori_loop(0, count - 1, step, 0, unroll=True)
+    half = group // 2
+    moves = [(a, b) for a in range(2) for b in range(half)]
+    moves = sorted(moves, key=lambda move: -(move[0] + min(move[1], half - move[1])))
+
+    def plane_others(body):
+        for a, b in moves:
+            if a + b:
+                body(lax.rem(j // half + a, 2) * half + lax.rem(lax.rem(j, half) + b, half))
+
+    def slice_others(body):
+        side, core = mine // 2, lax.rem(mine, 2)
+        rest = lax.rem(side + 1, shards // 2) * 2
+        body(rest + core)
+        body(rest + 1 - core)
+        body(side * 2 + 1 - core)
 
     def nearest(body):
-        lax.fori_loop(z + 1, jnp.minimum(z + NEAR, depth), lambda k, c: (body(k), c)[1], 0)
+        for d in range(1, NEAR):
+            pl.when(z + d < depth)(functools.partial(body, z + d))
 
     def greet(peer):
         pl.semaphore_signal(barrier, inc=1, device_id=peer, device_id_type=MESH)
@@ -62,8 +72,8 @@
 
     barrier = pltpu.get_barrier_semaphore()
     first_near = jnp.maximum(z - NEAR + 1, 0)
-    others(group, j, lambda q: greet(group_peer(q)))
-    others(shards, mine, lambda p: greet(space_peer(p)))
+    plane_others(lambda q: greet(group_peer(q)))
+    slice_others(lambda p: greet(space_peer(p)))
     lax.fori_loop(z + 1, jnp.minimum(z + NEAR + 1, depth), lambda k, c: (greet(z_peer(k)), c)[1], 0)
 
     loads = [
@@ -141,13 +151,13 @@
             src_ref=row_src, dst_ref=rows.at[mine], send_sem=row_send, recv_sem=row_recv,
             device_id=space_peer(p), device_id_type=MESH)
 
-    others(group, j, lambda q: rate_copy(q).start())
+    plane_others(lambda q: rate_copy(q).start())
     lax.fori_loop(
         0, jnp.minimum(z, NEAR),
         lambda k, c: (
             pl.semaphore_signal(ready.at[z], inc=1, device_id=z_peer(z - 1 - k), device_id_type=MESH), c)[1], 0)
-    others(shards, mine, lambda p: row_copy(p).start())
-    others(shards, mine, lambda p: full_copy(p).start())
+    slice_others(lambda p: row_copy(p).start())
+    slice_others(lambda p: full_copy(p).start())
     arrived(group_rates.at[pl.ds(0, group - 1)], rate_recv)
     total = jnp.zeros((1, 128), jnp.float32)
     before = jnp.zeros((1, 128), jnp.float32)
@@ -214,20 +224,31 @@
     def turn(value, by):
         return pltpu.roll(value.reshape(EY, EZ, 2 * DOF), by, 1).reshape(LAYER, 2 * DOF)
 
+    def advanced(value, after, before_it, value_decay, value_mass):
+        beside = jnp.where(low, after, before_it)
+        parts = [
+            value, beside, pltpu.roll(value, EZ, 0), pltpu.roll(value, LAYER - EZ, 0),
+            turn(value, 1), turn(value, EZ - 1),
+        ]
+        stacked = jnp.concatenate([part.astype(jnp.bfloat16) for part in parts], axis=1)
+        change = jnp.dot(stacked, blocks[...], preferred_element_type=jnp.float32)
+        return value_decay * value + value_mass * change
+
     def fine_step(step, carry):
         old = [state[p] for p in range(shards)]
         edge = jnp.zeros((LAYER, 2 * DOF), jnp.float32)
         for p in range(shards):
-            value = old[p]
-            beside = jnp.where(low, old[p + 1] if p + 1 < shards else edge, old[p - 1] if p else edge)
-            parts = [
-                value, beside, pltpu.roll(value, EZ, 0), pltpu.roll(value, LAYER - EZ, 0),
-                turn(value, 1), turn(value, EZ - 1),
-            ]
-            stacked = jnp.concatenate([part.astype(jnp.bfloat16) for part in parts], axis=1)
-            change = jnp.dot(stacked, blocks[...], preferred_element_type=jnp.float32)
-            state[p] = decay[p] * value + mass[p] * change
+            after = old[p + 1] if p + 1 < shards else edge
+            state[p] = advanced(old[p], after, old[p - 1] if p else edge, decay[p], mass[p])
         return carry
+
+    def at(ref, p):
+        return ref[pl.ds(p, 1)][0]
+
+    def last_step():
+        after = jnp.where(mine + 1 < shards, at(state, jnp.minimum(mine + 1, shards - 1)), 0.0)
+        before_it = jnp.where(mine > 0, at(state, jnp.maximum(mine - 1, 0)), 0.0)
+        return advanced(at(state, mine), after, before_it, at(decay, mine), at(mass, mine))
 
     def leave():
         def left(ref, sem):
@@ -260,8 +281,8 @@
 
     offset = None
     for it in range(ITERS):
-        lax.fori_loop(0, FINE, fine_step, 0, unroll=FINE)
-        offset = flat(state[pl.ds(mine, 1)][0]) - coarse[...] * start[...]
+        lax.fori_loop(0, FINE - 1, fine_step, 0, unroll=FINE - 1)
+        offset = flat(last_step()) - coarse[...] * start[...]
         off_src[it] = offset.reshape(group, OCTET, cells)
 
         def off_copy(q):
@@ -269,7 +290,7 @@
                 src_ref=off_src.at[it, q], dst_ref=offs.at[it, j], send_sem=off_send.at[it],
                 recv_sem=off_recv.at[it], device_id=group_peer(q), device_id_type=MESH)
 
-        others(group, j, lambda q: off_copy(q).start())
+        plane_others(lambda q: off_copy(q).start())
         offs[it, pl.ds(j, 1)] = off_src[it, pl.ds(j, 1)]
         if it == 0:
             def fill_gain(k, carry):
@@ -333,12 +354,12 @@
                 halo_src[it, q] = piece.astype(jnp.bfloat16)
 
             def fan(p):
-                others(group, j, lambda q: halo_copy(it, q, p).start())
+                plane_others(lambda q: halo_copy(it, q, p).start())
                 halo_copy(it, j, p).start()
 
-            others(shards, mine, fan)
-
-        others(group, j, lambda q: back_copy(q).start())
+            slice_others(fan)
+
+        plane_others(lambda q: back_copy(q).start())
         back[it, pl.ds(j, 1)] = back_src[it, pl.ds(j, 1)]
         if it + 1 == ITERS:
             leave()

time: 49.4 us -> 49 us (level)
  no operation moved by 1% of the time
where the time goes in v7:
time: 49 us; the launch traced here: 48.9 us
  Pallas kernels  47.5 us (97%)
  other arithmetic  0.66 us (1%)
  between operations  0.64 us (1%)
    pallas_call x1, Pallas kernels, per_device(): pl.pallas_call(functools.partial(kernel, depth, group, shards), out_shape...  47.5 us

profile of v7, /device:TPU:480, one launch (start us, length us, event | category | flops | bytes accessed | tf_op | source)
XLA Modules:
  0.0 48.9 jit_solution(7307722175624402432)
XLA Ops:
  0.6 47.5 %parareal.1 = (f32[64,256]{1,0:T(8,128)S(1)}, f32[64,256]{1,0:T(8,128)S(1)}) custom-call(f32[64,256]{1,0:T(8,128)} %init_hbm.1, f32[1,256]{1,0:T(1,128)} %bitcast.6, f32[1,256]{1,0:T(1,128)} %bitcast.7, f32[1,64]{1,0:T(1,128)} %rate_hbm.1, bf16[64,64]{1,0:T(8,128)(2,1)} %volume_hbm.1, bf16[6,64,64]{2,1,0:T(8,128)(2,1)} %faces_hbm.1), custom_call_target="tpu_custom_call" | custom-call | tf_op jit(solution)/shard_map/parareal/pallas_call | solution.py:391
  48.2 0.7 %subtract_bitcast_fusion = (f32[1,64,256]{2,1,0:T(8,128)}, f32[1,64,256]{2,1,0:T(8,128)}) fusion(f32[64,256]{1,0:T(8,128)S(1)} %get-tuple-element.4, f32[64,256]{1,0:T(8,128)S(1)} %get-tuple-element.5), kind=kLoop, calls=%fused_computation | loop fusion | flops 32768 | bytes 262144 | tf_op jit(solution)/shard_map/broadcast_in_dim | solution.py:440

commit v8 on v7

--- a/solution.py
+++ b/solution.py
@@ -151,11 +151,11 @@
             src_ref=row_src, dst_ref=rows.at[mine], send_sem=row_send, recv_sem=row_recv,
             device_id=space_peer(p), device_id_type=MESH)
 
-    plane_others(lambda q: rate_copy(q).start())
     lax.fori_loop(
         0, jnp.minimum(z, NEAR),
         lambda k, c: (
             pl.semaphore_signal(ready.at[z], inc=1, device_id=z_peer(z - 1 - k), device_id_type=MESH), c)[1], 0)
+    plane_others(lambda q: rate_copy(q).start())
     slice_others(lambda p: row_copy(p).start())
     slice_others(lambda p: full_copy(p).start())
     arrived(group_rates.at[pl.ds(0, group - 1)], rate_recv)

time: 49 us -> 49 us (level)
  no operation moved by 1% of the time
where the time goes in v8:
time: 49 us; the launch traced here: 48.9 us
  Pallas kernels  47.6 us (97%)
  other arithmetic  0.66 us (1%)
  between operations  0.64 us (1%)
    pallas_call x1, Pallas kernels, per_device(): pl.pallas_call(functools.partial(kernel, depth, group, shards), out_shape...  47.6 us

profile of v8, /device:TPU:480, one launch (start us, length us, event | category | flops | bytes accessed | tf_op | source)
XLA Modules:
  0.0 48.9 jit_solution(13883704735147055323)
XLA Ops:
  0.6 47.6 %parareal.1 = (f32[64,256]{1,0:T(8,128)S(1)}, f32[64,256]{1,0:T(8,128)S(1)}) custom-call(f32[64,256]{1,0:T(8,128)} %init_hbm.1, f32[1,256]{1,0:T(1,128)} %bitcast.6, f32[1,256]{1,0:T(1,128)} %bitcast.7, f32[1,64]{1,0:T(1,128)} %rate_hbm.1, bf16[64,64]{1,0:T(8,128)(2,1)} %volume_hbm.1, bf16[6,64,64]{2,1,0:T(8,128)(2,1)} %faces_hbm.1), custom_call_target="tpu_custom_call" | custom-call | tf_op jit(solution)/shard_map/parareal/pallas_call | solution.py:391
  48.2 0.7 %subtract_bitcast_fusion = (f32[1,64,256]{2,1,0:T(8,128)}, f32[1,64,256]{2,1,0:T(8,128)}) fusion(f32[64,256]{1,0:T(8,128)S(1)} %get-tuple-element.4, f32[64,256]{1,0:T(8,128)S(1)} %get-tuple-element.5), kind=kLoop, calls=%fused_computation | loop fusion | flops 32768 | bytes 262144 | tf_op jit(solution)/shard_map/broadcast_in_dim | solution.py:440
